TPU v7x, 512 devices: a whole 4x4x16 slice. The times are simulated.
512 devices in a mesh: bx: 32 (over z, core), by: 16 (over y, x).
Axes of the slice: x: 4, y: 4, z: 16, core: 2. Of those that a mesh axis runs over, the one named last changes fastest.
Arguments:
- rhs: float32 [256, 128, 256], P('bx', 'by'), may hold values from -5 to 6.5
- acoef: float32 [256, 128, 256], P('bx', 'by'), may hold values from 0.02 to 0.4
- beta_x: float32 [256, 128, 256], P('bx', 'by'), may hold values from 0.5 to 2
- beta_y: float32 [256, 128, 256], P('bx', 'by'), may hold values from 0.5 to 2
- beta_z: float32 [256, 128, 256], P('bx', 'by'), may hold values from 0.5 to 2
Outputs:
- solution: float32 [256, 128, 256], P('bx', 'by')
All inputs are finite; a program needn't handle non-finite values.
Results may differ from a plain program's by a relative error of at most 0.0001.
Values sent between devices are 32-bit elements; how exact they have to be, the bound alone decides.
A program may use at most 64 MiB of HBM per device.

v0:
```python
import jax
import jax.numpy as jnp
from jax import lax
from jax.sharding import PartitionSpec as P

LEVELS = 3
PRE = 3
POST = 3
COARSE = 8


damping = 0.8


def passed_along(value, axis, steps):
    count = lax.axis_size(axis)
    initial, last = (max(0, -steps), min(count, count - steps))
    return lax.ppermute(value, axis, [(source, source + steps) for source in range(initial, last)])


def partner(value, axis, stride):
    mask = 2**stride
    pairs = [(source, source ^ mask) for source in range(lax.axis_size(axis))]
    return lax.ppermute(value, axis, pairs)


def restrict_cells(values):
    size_x, size_y, size_z = values.shape
    blocks = values.reshape(size_x // 2, 2, size_y // 2, 2, size_z // 2, 2)
    return blocks.sum(axis=(1, 3, 5)) * 0.125


def coarse_faces(beta, axis_no):
    size_x, size_y, size_z = beta.shape
    blocks = beta.reshape(size_x // 2, 2, size_y // 2, 2, size_z // 2, 2)
    if axis_no == 0:
        picked = blocks[:, 0, :, :, :, :].sum(axis=(2, 4))
    elif axis_no == 1:
        picked = blocks[:, :, :, 0, :, :].sum(axis=(1, 4))
    else:
        picked = blocks[:, :, :, :, :, 0].sum(axis=(1, 3))
    return picked * 0.0625


def prolong(values):
    size_x, size_y, size_z = values.shape
    spread = jnp.broadcast_to(values[:, None, :, None, :, None], (size_x, 2, size_y, 2, size_z, 2))
    return spread.reshape(2 * size_x, 2 * size_y, 2 * size_z)


def along_x(values, offset):
    return passed_along(values, "bx", offset)


def along_y(values, offset):
    return passed_along(values, "by", offset)


def neighbours(values, spacing_x, spacing_y):
    size_x, size_y, size_z = values.shape
    lower_x = jnp.concatenate(
        [along_x(values[size_x - 1 :], spacing_x), values[: size_x - 1]], axis=0
    )
    upper_x = jnp.concatenate([values[1:], along_x(values[:1], -spacing_x)], axis=0)
    lower_y = jnp.concatenate(
        [along_y(values[:, size_y - 1 :], spacing_y), values[:, : size_y - 1]], axis=1
    )
    upper_y = jnp.concatenate([values[:, 1:], along_y(values[:, :1], -spacing_y)], axis=1)
    zero_plane = jnp.zeros((size_x, size_y, 1), values.dtype)
    lower_z = jnp.concatenate([zero_plane, values[:, :, : size_z - 1]], axis=2)
    upper_z = jnp.concatenate([values[:, :, 1:], zero_plane], axis=2)
    return (lower_x, upper_x, lower_y, upper_y, lower_z, upper_z)


def build(cell_coef, face_x, face_y, face_z, spacing_x, spacing_y):
    high_x = jnp.concatenate([face_x[1:], along_x(face_x[:1], -spacing_x)], axis=0)
    high_y = jnp.concatenate([face_y[:, 1:], along_y(face_y[:, :1], -spacing_y)], axis=1)
    zero_plane = jnp.zeros((face_z.shape[0], face_z.shape[1], 1), face_z.dtype)
    high_z = jnp.concatenate([face_z[:, :, 1:], zero_plane], axis=2)
    diag = cell_coef + face_x + high_x + face_y + high_y + face_z + high_z
    return (cell_coef, face_x, high_x, face_y, high_y, face_z, high_z, diag)


def apply_op(values, coeffs, spacing_x, spacing_y):
    lower_x, upper_x, lower_y, upper_y, lower_z, upper_z = neighbours(values, spacing_x, spacing_y)
    result = coeffs[7] * values - coeffs[1] * lower_x - coeffs[2] * upper_x
    result = result - coeffs[3] * lower_y - coeffs[4] * upper_y
    result = result - coeffs[5] * lower_z - coeffs[6] * upper_z
    return result


def smooth(values, source, coeffs, sweeps, spacing_x, spacing_y):
    for sweep_no in range(sweeps):
        values = (
            values + damping * (source - apply_op(values, coeffs, spacing_x, spacing_y)) / coeffs[7]
        )
    return values


def joined(local_set, partner_set, is_first, axis_no):
    return tuple(
        (
            jnp.where(
                is_first,
                jnp.concatenate([own_block, far_block], axis=axis_no),
                jnp.concatenate([far_block, own_block], axis=axis_no),
            )
            for own_block, far_block in zip(local_set, partner_set)
        )
    )


def merge_x(source, cell_coef, face_x, face_y, face_z, bit_no):
    partner_set = partner((source, cell_coef, face_x, face_y, face_z), "bx", bit_no)
    is_first = lax.axis_index("bx") // 2**bit_no % 2 == 0
    return joined((source, cell_coef, face_x, face_y, face_z), partner_set, is_first, 0)


def merge_y(source, cell_coef, face_x, face_y, face_z, bit_no):
    partner_set = partner((source, cell_coef, face_x, face_y, face_z), "by", bit_no)
    is_first = lax.axis_index("by") // 2**bit_no % 2 == 0
    return joined((source, cell_coef, face_x, face_y, face_z), partner_set, is_first, 1)


def own_half(values, axis_tag, bit_no):
    if axis_tag == "x":
        half_size = values.shape[0] // 2
        start = lax.axis_index("bx") // 2**bit_no % 2 * half_size
        return lax.dynamic_slice_in_dim(values, start, half_size, 0)
    half_size = values.shape[1] // 2
    start = lax.axis_index("by") // 2**bit_no % 2 * half_size
    return lax.dynamic_slice_in_dim(values, start, half_size, 1)


def body(rhs, acoef, beta_x, beta_y, beta_z):
    joins = [("x" if level_no % 2 == 0 else "y", level_no // 2) for level_no in range(LEVELS)]
    plan = [[entry] for entry in joins]
    spacing_x, spacing_y = (1, 1)
    source = rhs
    cell_coef, face_x, face_y, face_z = (acoef, beta_x, beta_y, beta_z)
    stored = []
    for level_no in range(LEVELS):
        coeffs = build(cell_coef, face_x, face_y, face_z, spacing_x, spacing_y)
        values = damping * source / coeffs[7]
        values = smooth(values, source, coeffs, PRE - 1, spacing_x, spacing_y)
        remains = source - apply_op(values, coeffs, spacing_x, spacing_y)
        stored.append((values, source, coeffs, spacing_x, spacing_y))
        source = restrict_cells(remains)
        cell_coef = restrict_cells(cell_coef)
        face_x = coarse_faces(face_x, 0)
        face_y = coarse_faces(face_y, 1)
        face_z = coarse_faces(face_z, 2)
        for axis_tag, bit_no in plan[level_no]:
            if axis_tag == "x":
                source, cell_coef, face_x, face_y, face_z = merge_x(
                    source, cell_coef, face_x, face_y, face_z, bit_no
                )
                spacing_x = spacing_x * 2
            else:
                source, cell_coef, face_x, face_y, face_z = merge_y(
                    source, cell_coef, face_x, face_y, face_z, bit_no
                )
                spacing_y = spacing_y * 2
    coeffs = build(cell_coef, face_x, face_y, face_z, spacing_x, spacing_y)
    values = damping * source / coeffs[7]
    values = smooth(values, source, coeffs, COARSE - 1, spacing_x, spacing_y)
    for level_no in reversed(range(LEVELS)):
        for axis_tag, bit_no in reversed(plan[level_no]):
            values = own_half(values, axis_tag, bit_no)
        fine_values, fine_source, fine_coeffs, fine_sx, fine_sy = stored[level_no]
        values = fine_values + prolong(values)
        values = smooth(values, fine_source, fine_coeffs, POST, fine_sx, fine_sy)
    return values


def solution(mesh):
    placed = (
        P("bx", "by", None),
        P("bx", "by", None),
        P("bx", "by", None),
        P("bx", "by", None),
        P("bx", "by", None),
    )
    return jax.shard_map(
        body, mesh=mesh, in_specs=placed, out_specs=P("bx", "by", None), check_vma=False
    )
```

profile of v0, /device:TPU:398, one launch (start us, length us, event | category | flops | bytes accessed | tf_op | source)
XLA Modules:
  0.0 555.9 jit_solution(141096219178582931)
XLA Ops:
  8.0 6.3 %reshape.77 = f32[4,2,4,2,128,2]{5,4,3,2,1,0:T(8,128)} reshape(f32[8,8,256]{2,1,0:T(8,128)} %param.9) | data formatting | bytes 131072 | tf_op jit(solution)/shard_map/reshape | solution.py:35
  18.8 5.6 %reshape.76 = f32[4,2,4,2,128,2]{5,4,3,2,1,0:T(8,128)} reshape(f32[8,8,256]{2,1,0:T(8,128)S(1)} %copy-done) | data formatting | bytes 131072 | tf_op jit(solution)/shard_map/reshape | solution.py:35
  28.8 5.6 %reshape.75 = f32[4,2,4,2,128,2]{5,4,3,2,1,0:T(8,128)} reshape(f32[8,8,256]{2,1,0:T(8,128)S(1)} %copy-done.1) | data formatting | bytes 131072 | tf_op jit(solution)/shard_map/reshape | solution.py:35
  38.4 5.6 %reshape.74 = f32[4,2,4,2,128,2]{5,4,3,2,1,0:T(8,128)} reshape(f32[8,8,256]{2,1,0:T(8,128)S(1)} %copy-done.3) | data formatting | bytes 131072 | tf_op jit(solution)/shard_map/reshape | solution.py:29
  49.4 5.2 collective-permute-start.4
  62.2 4.9 collective-permute-start.3
  93.3 4.9 collective-permute-start.7
  109.9 4.9 collective-permute-start.11
  129.4 5.6 %reshape.73 = f32[4,2,4,2,128,2]{5,4,3,2,1,0:T(8,128)} reshape(f32[8,8,256]{2,1,0:T(8,128)S(1)} %fusion.26) | data formatting | bytes 131072 | tf_op jit(solution)/shard_map/reshape | solution.py:29
  159.4 6.0 %collective-permute-start.27 = (f32[8,1,128]{2,1,0:T(1,128)S(1)}, f32[8,1,128]{2,1,0:T(1,128)S(1)}, u32[]{:S(2)}, u32[]{:S(2)}) collective-permute-start(f32[8,1,128]{2,1,0:T(1,128)S(1)} %get-tuple-element.120), channel_id=1, source_target_pairs={{0,1},{1,2},{2,3},{3,4},{4,5},{5,6},{6,7},{7,8},{8,9},{9,10},{10,1... | collective-permute-start | bytes 12296 | tf_op jit(solution)/shard_map/ppermute | solution.py:18
  206.5 6.3 %collective-permute-start.42 = (f32[4,1,64]{2,0,1:T(4,128)S(1)}, f32[4,1,64]{2,0,1:T(4,128)S(1)}, u32[]{:S(2)}, u32[]{:S(2)}) collective-permute-start(f32[4,1,64]{2,0,1:T(4,128)S(1)} %get-tuple-element.190), channel_id=1, source_target_pairs={{0,2},{1,3},{2,4},{3,5},{4,6},{5,7},{6,8},{7,9},{8,10},{9,11},{10,... | collective-permute-start | bytes 3080 | tf_op jit(solution)/shard_map/ppermute | solution.py:18
  223.6 6.3 %collective-permute-start.46 = (f32[4,1,64]{2,0,1:T(4,128)S(1)}, f32[4,1,64]{2,0,1:T(4,128)S(1)}, u32[]{:S(2)}, u32[]{:S(2)}) collective-permute-start(f32[4,1,64]{2,0,1:T(4,128)S(1)} %get-tuple-element.180), channel_id=1, source_target_pairs={{0,2},{1,3},{2,4},{3,5},{4,6},{5,7},{6,8},{7,9},{8,10},{9,11},{10,... | collective-permute-start | bytes 3080 | tf_op jit(solution)/shard_map/ppermute | solution.py:18
  269.3 5.5 collective-permute-start.61
  287.0 6.3 %collective-permute-start.65 = (f32[4,1,32]{2,1,0:T(1,128)S(1)}, f32[4,1,32]{2,1,0:T(1,128)S(1)}, u32[]{:S(2)}, u32[]{:S(2)}) collective-permute-start(f32[4,1,32]{2,1,0:T(1,128)S(1)} %get-tuple-element.240), channel_id=1, source_target_pairs={{0,2},{1,3},{2,4},{3,5},{4,6},{5,7},{6,8},{7,9},{8,10},{9,11},{10,... | collective-permute-start | bytes 1544 | tf_op jit(solution)/shard_map/ppermute | solution.py:18
  305.2 6.3 %collective-permute-start.69 = (f32[4,1,32]{2,1,0:T(1,128)S(1)}, f32[4,1,32]{2,1,0:T(1,128)S(1)}, u32[]{:S(2)}, u32[]{:S(2)}) collective-permute-start(f32[4,1,32]{2,1,0:T(1,128)S(1)} %get-tuple-element.232), channel_id=1, source_target_pairs={{0,2},{1,3},{2,4},{3,5},{4,6},{5,7},{6,8},{7,9},{8,10},{9,11},{10,... | collective-permute-start | bytes 1544 | tf_op jit(solution)/shard_map/ppermute | solution.py:18
  323.1 6.3 %collective-permute-start.73 = (f32[4,1,32]{2,1,0:T(1,128)S(1)}, f32[4,1,32]{2,1,0:T(1,128)S(1)}, u32[]{:S(2)}, u32[]{:S(2)}) collective-permute-start(f32[4,1,32]{2,1,0:T(1,128)S(1)} %get-tuple-element.224), channel_id=1, source_target_pairs={{0,2},{1,3},{2,4},{3,5},{4,6},{5,7},{6,8},{7,9},{8,10},{9,11},{10,... | collective-permute-start | bytes 1544 | tf_op jit(solution)/shard_map/ppermute | solution.py:18
  341.0 6.3 %collective-permute-start.77 = (f32[4,1,32]{2,1,0:T(1,128)S(1)}, f32[4,1,32]{2,1,0:T(1,128)S(1)}, u32[]{:S(2)}, u32[]{:S(2)}) collective-permute-start(f32[4,1,32]{2,1,0:T(1,128)S(1)} %get-tuple-element.216), channel_id=1, source_target_pairs={{0,2},{1,3},{2,4},{3,5},{4,6},{5,7},{6,8},{7,9},{8,10},{9,11},{10,... | collective-permute-start | bytes 1544 | tf_op jit(solution)/shard_map/ppermute | solution.py:18
  359.0 6.3 %collective-permute-start.81 = (f32[4,1,32]{2,1,0:T(1,128)S(1)}, f32[4,1,32]{2,1,0:T(1,128)S(1)}, u32[]{:S(2)}, u32[]{:S(2)}) collective-permute-start(f32[4,1,32]{2,1,0:T(1,128)S(1)} %get-tuple-element.208), channel_id=1, source_target_pairs={{0,2},{1,3},{2,4},{3,5},{4,6},{5,7},{6,8},{7,9},{8,10},{9,11},{10,... | collective-permute-start | bytes 1544 | tf_op jit(solution)/shard_map/ppermute | solution.py:18
  397.7 5.2 collective-permute-start.89
  414.2 6.1 %collective-permute-start.93 = (f32[4,1,64]{2,0,1:T(4,128)S(1)}, f32[4,1,64]{2,0,1:T(4,128)S(1)}, u32[]{:S(2)}, u32[]{:S(2)}) collective-permute-start(f32[4,1,64]{2,0,1:T(4,128)S(1)} %get-tuple-element.150), channel_id=1, source_target_pairs={{0,2},{1,3},{2,4},{3,5},{4,6},{5,7},{6,8},{7,9},{8,10},{9,11},{10,... | collective-permute-start | bytes 3080 | tf_op jit(solution)/shard_map/ppermute | solution.py:18
  450.8 5.7 %collective-permute-start.101 = (f32[8,1,128]{2,1,0:T(1,128)S(1)}, f32[8,1,128]{2,1,0:T(1,128)S(1)}, u32[]{:S(2)}, u32[]{:S(2)}) collective-permute-start(f32[8,1,128]{2,1,0:T(1,128)S(1)} %get-tuple-element.100), channel_id=1, source_target_pairs={{0,1},{1,2},{2,3},{3,4},{4,5},{5,6},{6,7},{7,8},{8,9},{9,10},{10,1... | collective-permute-start | bytes 12296 | tf_op jit(solution)/shard_map/ppermute | solution.py:18
  467.3 6.0 %collective-permute-start.105 = (f32[8,1,128]{2,1,0:T(1,128)S(1)}, f32[8,1,128]{2,1,0:T(1,128)S(1)}, u32[]{:S(2)}, u32[]{:S(2)}) collective-permute-start(f32[8,1,128]{2,1,0:T(1,128)S(1)} %get-tuple-element.90), channel_id=1, source_target_pairs={{0,1},{1,2},{2,3},{3,4},{4,5},{5,6},{6,7},{7,8},{8,9},{9,10},{10,1... | collective-permute-start | bytes 12296 | tf_op jit(solution)/shard_map/ppermute | solution.py:18
  507.5 4.9 collective-permute-start.112
  524.1 4.9 collective-permute-start.116
  (477 shorter events, 416.4 us)
Async XLA Ops:
  0.7 46.0 %collective-permute-start = (f32[1,8,256]{2,1,0:T(8,128)S(1)}, f32[1,8,256]{2,1,0:T(8,128)S(1)}, u32[]{:S(2)}, u32[]{:S(2)}) collective-permute-start(f32[1,8,256]{2,1,0:T(8,128)S(1)} %slice.810), channel_id=1, source_target_pairs={{16,0},{32,16},{48,32},{64,48},{80,64},{96,80},{112,96},{128,112},... | collective-permute-start | bytes 24584 | tf_op jit(solution)/shard_map/ppermute | solution.py:18
  5.1 44.0 %collective-permute-start.1 = (f32[8,1,256]{2,1,0:T(1,128)S(1)}, f32[8,1,256]{2,1,0:T(1,128)S(1)}, u32[]{:S(2)}, u32[]{:S(2)}) collective-permute-start(f32[8,1,256]{2,1,0:T(1,128)S(1)} %slice.812), channel_id=1, source_target_pairs={{1,0},{2,1},{3,2},{4,3},{5,4},{6,5},{7,6},{8,7},{9,8},{10,9},{11,1... | collective-permute-start | bytes 24584 | tf_op jit(solution)/shard_map/ppermute | solution.py:18
  16.9 37.8 %collective-permute-start.20 = (f32[4,4,128]{2,1,0:T(4,128)S(1)}, f32[4,4,128]{2,1,0:T(4,128)S(1)}, u32[]{:S(2)}, u32[]{:S(2)}) collective-permute-start(f32[4,4,128]{2,1,0:T(4,128)S(1)} %broadcast_multiply_fusion), channel_id=1, source_target_pairs={{0,16},{16,0},{32,48},{48,32},{64,80},{80,64},{96,112},{112,96},{1... | collective-permute-start | bytes 24584 | tf_op jit(solution)/shard_map/ppermute | solution.py:24
  26.3 31.4 %collective-permute-start.18 = (f32[4,4,128]{2,1,0:T(4,128)S(1)}, f32[4,4,128]{2,1,0:T(4,128)S(1)}, u32[]{:S(2)}, u32[]{:S(2)}) collective-permute-start(f32[4,4,128]{2,1,0:T(4,128)S(1)} %broadcast_multiply_fusion.1), channel_id=1, source_target_pairs={{0,16},{16,0},{32,48},{48,32},{64,80},{80,64},{96,112},{112,96},{1... | collective-permute-start | bytes 24584 | tf_op jit(solution)/shard_map/ppermute | solution.py:24
  46.7 92.7 %collective-permute-start.15 = (f32[4,4,128]{2,1,0:T(4,128)S(1)}, f32[4,4,128]{2,1,0:T(4,128)S(1)}, u32[]{:S(2)}, u32[]{:S(2)}) collective-permute-start(f32[4,4,128]{2,1,0:T(4,128)S(1)} %broadcast_multiply_fusion.3), channel_id=1, source_target_pairs={{0,16},{16,0},{32,48},{48,32},{64,80},{80,64},{96,112},{112,96},{1... | collective-permute-start | bytes 24584 | tf_op jit(solution)/shard_map/ppermute | solution.py:24
  49.4 38.1 %collective-permute-start.4 = (f32[8,1,256]{2,1,0:T(1,128)S(1)}, f32[8,1,256]{2,1,0:T(1,128)S(1)}, u32[]{:S(2)}, u32[]{:S(2)}) collective-permute-start(f32[8,1,256]{2,1,0:T(1,128)S(1)} %get-tuple-element.71), channel_id=1, source_target_pairs={{0,1},{1,2},{2,3},{3,4},{4,5},{5,6},{6,7},{7,8},{8,9},{9,10},{10,1... | collective-permute-start | bytes 24584 | tf_op jit(solution)/shard_map/ppermute | solution.py:18
  60.2 27.2 %collective-permute-start.2 = (f32[1,8,256]{2,1,0:T(8,128)S(1)}, f32[1,8,256]{2,1,0:T(8,128)S(1)}, u32[]{:S(2)}, u32[]{:S(2)}) collective-permute-start(f32[1,8,256]{2,1,0:T(8,128)S(1)} %get-tuple-element.75), channel_id=1, source_target_pairs={{0,16},{16,32},{32,48},{48,64},{64,80},{80,96},{96,112},{112,128},... | collective-permute-start | bytes 24584 | tf_op jit(solution)/shard_map/ppermute | solution.py:18
  62.2 25.3 %collective-permute-start.3 = (f32[1,8,256]{2,1,0:T(8,128)S(1)}, f32[1,8,256]{2,1,0:T(8,128)S(1)}, u32[]{:S(2)}, u32[]{:S(2)}) collective-permute-start(f32[1,8,256]{2,1,0:T(8,128)S(1)} %get-tuple-element.74), channel_id=1, source_target_pairs={{16,0},{32,16},{48,32},{64,48},{80,64},{96,80},{112,96},{128,112},... | collective-permute-start | bytes 24584 | tf_op jit(solution)/shard_map/ppermute | solution.py:18
  120.7 18.7 %collective-permute-start.19 = (f32[8,1,128]{2,1,0:T(1,128)S(1)}, f32[8,1,128]{2,1,0:T(1,128)S(1)}, u32[]{:S(2)}, u32[]{:S(2)}) collective-permute-start(f32[8,1,128]{2,1,0:T(1,128)S(1)} %slice.1109), channel_id=1, source_target_pairs={{1,0},{2,1},{3,2},{4,3},{5,4},{6,5},{7,6},{8,7},{9,8},{10,9},{11,1... | collective-permute-start | bytes 12296 | tf_op jit(solution)/shard_map/ppermute | solution.py:18
  122.6 16.8 %collective-permute-start.17 = (f32[1,4,128]{2,1,0:T(4,128)S(1)}, f32[1,4,128]{2,1,0:T(4,128)S(1)}, u32[]{:S(2)}, u32[]{:S(2)}) collective-permute-start(f32[1,4,128]{2,1,0:T(4,128)S(1)} %slice.1106), channel_id=1, source_target_pairs={{32,0},{48,16},{64,32},{80,48},{96,64},{112,80},{128,96},{144,112}... | collective-permute-start | bytes 6152 | tf_op jit(solution)/shard_map/ppermute | solution.py:18
  124.6 78.0 %collective-permute-start.38 = (f32[4,1,64]{2,0,1:T(4,128)S(1)}, f32[4,1,64]{2,0,1:T(4,128)S(1)}, u32[]{:S(2)}, u32[]{:S(2)}) collective-permute-start(f32[4,1,64]{2,0,1:T(4,128)S(1)} %slice.1147), channel_id=1, source_target_pairs={{2,0},{3,1},{4,2},{5,3},{6,4},{7,5},{8,6},{9,7},{10,8},{11,9},{12,... | collective-permute-start | bytes 3080 | tf_op jit(solution)/shard_map/ppermute | solution.py:18
  140.7 16.6 %collective-permute-start.24 = (f32[8,1,128]{2,1,0:T(1,128)S(1)}, f32[8,1,128]{2,1,0:T(1,128)S(1)}, u32[]{:S(2)}, u32[]{:S(2)}) collective-permute-start(f32[8,1,128]{2,1,0:T(1,128)S(1)} %get-tuple-element.131), channel_id=1, source_target_pairs={{1,0},{2,1},{3,2},{4,3},{5,4},{6,5},{7,6},{8,7},{9,8},{10,9},{11,1... | collective-permute-start | bytes 12296 | tf_op jit(solution)/shard_map/ppermute | solution.py:18
  157.5 16.9 %collective-permute-start.28 = (f32[8,1,128]{2,1,0:T(1,128)S(1)}, f32[8,1,128]{2,1,0:T(1,128)S(1)}, u32[]{:S(2)}, u32[]{:S(2)}) collective-permute-start(f32[8,1,128]{2,1,0:T(1,128)S(1)} %get-tuple-element.121), channel_id=1, source_target_pairs={{1,0},{2,1},{3,2},{4,3},{5,4},{6,5},{7,6},{8,7},{9,8},{10,9},{11,1... | collective-permute-start | bytes 12296 | tf_op jit(solution)/shard_map/ppermute | solution.py:18
  189.5 73.8 %collective-permute-start.58 = (f32[2,2,32]{2,1,0:T(2,128)S(1)}, f32[2,2,32]{2,1,0:T(2,128)S(1)}, u32[]{:S(2)}, u32[]{:S(2)}) collective-permute-start(f32[2,2,32]{2,1,0:T(2,128)S(1)} %broadcast_multiply_fusion.10), channel_id=1, source_target_pairs={{0,32},{16,48},{32,0},{48,16},{64,96},{80,112},{96,64},{112,80},{1... | collective-permute-start | bytes 1544 | tf_op jit(solution)/shard_map/ppermute | solution.py:24
  266.5 18.4 %collective-permute-start.62 = (f32[4,1,32]{2,1,0:T(1,128)S(1)}, f32[4,1,32]{2,1,0:T(1,128)S(1)}, u32[]{:S(2)}, u32[]{:S(2)}) collective-permute-start(f32[4,1,32]{2,1,0:T(1,128)S(1)} %get-tuple-element.249), channel_id=1, source_target_pairs={{2,0},{3,1},{4,2},{5,3},{6,4},{7,5},{8,6},{9,7},{10,8},{11,9},{12,... | collective-permute-start | bytes 1544 | tf_op jit(solution)/shard_map/ppermute | solution.py:18
  285.1 18.0 %collective-permute-start.66 = (f32[4,1,32]{2,1,0:T(1,128)S(1)}, f32[4,1,32]{2,1,0:T(1,128)S(1)}, u32[]{:S(2)}, u32[]{:S(2)}) collective-permute-start(f32[4,1,32]{2,1,0:T(1,128)S(1)} %get-tuple-element.241), channel_id=1, source_target_pairs={{2,0},{3,1},{4,2},{5,3},{6,4},{7,5},{8,6},{9,7},{10,8},{11,9},{12,... | collective-permute-start | bytes 1544 | tf_op jit(solution)/shard_map/ppermute | solution.py:18
  287.0 16.1 %collective-permute-start.65 = (f32[4,1,32]{2,1,0:T(1,128)S(1)}, f32[4,1,32]{2,1,0:T(1,128)S(1)}, u32[]{:S(2)}, u32[]{:S(2)}) collective-permute-start(f32[4,1,32]{2,1,0:T(1,128)S(1)} %get-tuple-element.240), channel_id=1, source_target_pairs={{0,2},{1,3},{2,4},{3,5},{4,6},{5,7},{6,8},{7,9},{8,10},{9,11},{10,... | collective-permute-start | bytes 1544 | tf_op jit(solution)/shard_map/ppermute | solution.py:18
  303.2 17.8 %collective-permute-start.70 = (f32[4,1,32]{2,1,0:T(1,128)S(1)}, f32[4,1,32]{2,1,0:T(1,128)S(1)}, u32[]{:S(2)}, u32[]{:S(2)}) collective-permute-start(f32[4,1,32]{2,1,0:T(1,128)S(1)} %get-tuple-element.233), channel_id=1, source_target_pairs={{2,0},{3,1},{4,2},{5,3},{6,4},{7,5},{8,6},{9,7},{10,8},{11,9},{12,... | collective-permute-start | bytes 1544 | tf_op jit(solution)/shard_map/ppermute | solution.py:18
  305.2 15.8 %collective-permute-start.69 = (f32[4,1,32]{2,1,0:T(1,128)S(1)}, f32[4,1,32]{2,1,0:T(1,128)S(1)}, u32[]{:S(2)}, u32[]{:S(2)}) collective-permute-start(f32[4,1,32]{2,1,0:T(1,128)S(1)} %get-tuple-element.232), channel_id=1, source_target_pairs={{0,2},{1,3},{2,4},{3,5},{4,6},{5,7},{6,8},{7,9},{8,10},{9,11},{10,... | collective-permute-start | bytes 1544 | tf_op jit(solution)/shard_map/ppermute | solution.py:18
  321.2 17.8 %collective-permute-start.74 = (f32[4,1,32]{2,1,0:T(1,128)S(1)}, f32[4,1,32]{2,1,0:T(1,128)S(1)}, u32[]{:S(2)}, u32[]{:S(2)}) collective-permute-start(f32[4,1,32]{2,1,0:T(1,128)S(1)} %get-tuple-element.225), channel_id=1, source_target_pairs={{2,0},{3,1},{4,2},{5,3},{6,4},{7,5},{8,6},{9,7},{10,8},{11,9},{12,... | collective-permute-start | bytes 1544 | tf_op jit(solution)/shard_map/ppermute | solution.py:18
  339.1 17.8 %collective-permute-start.78 = (f32[4,1,32]{2,1,0:T(1,128)S(1)}, f32[4,1,32]{2,1,0:T(1,128)S(1)}, u32[]{:S(2)}, u32[]{:S(2)}) collective-permute-start(f32[4,1,32]{2,1,0:T(1,128)S(1)} %get-tuple-element.217), channel_id=1, source_target_pairs={{2,0},{3,1},{4,2},{5,3},{6,4},{7,5},{8,6},{9,7},{10,8},{11,9},{12,... | collective-permute-start | bytes 1544 | tf_op jit(solution)/shard_map/ppermute | solution.py:18
  357.0 17.8 %collective-permute-start.82 = (f32[4,1,32]{2,1,0:T(1,128)S(1)}, f32[4,1,32]{2,1,0:T(1,128)S(1)}, u32[]{:S(2)}, u32[]{:S(2)}) collective-permute-start(f32[4,1,32]{2,1,0:T(1,128)S(1)} %get-tuple-element.209), channel_id=1, source_target_pairs={{2,0},{3,1},{4,2},{5,3},{6,4},{7,5},{8,6},{9,7},{10,8},{11,9},{12,... | collective-permute-start | bytes 1544 | tf_op jit(solution)/shard_map/ppermute | solution.py:18
  448.5 16.6 %collective-permute-start.102 = (f32[8,1,128]{2,1,0:T(1,128)S(1)}, f32[8,1,128]{2,1,0:T(1,128)S(1)}, u32[]{:S(2)}, u32[]{:S(2)}) collective-permute-start(f32[8,1,128]{2,1,0:T(1,128)S(1)} %get-tuple-element.101), channel_id=1, source_target_pairs={{1,0},{2,1},{3,2},{4,3},{5,4},{6,5},{7,6},{8,7},{9,8},{10,9},{11,1... | collective-permute-start | bytes 12296 | tf_op jit(solution)/shard_map/ppermute | solution.py:18
  465.3 16.6 %collective-permute-start.106 = (f32[8,1,128]{2,1,0:T(1,128)S(1)}, f32[8,1,128]{2,1,0:T(1,128)S(1)}, u32[]{:S(2)}, u32[]{:S(2)}) collective-permute-start(f32[8,1,128]{2,1,0:T(1,128)S(1)} %get-tuple-element.91), channel_id=1, source_target_pairs={{1,0},{2,1},{3,2},{4,3},{5,4},{6,5},{7,6},{8,7},{9,8},{10,9},{11,1... | collective-permute-start | bytes 12296 | tf_op jit(solution)/shard_map/ppermute | solution.py:18
  (104 other events, 1008.1 us)
where the time goes:
time: 560 us; the launch traced here: 556 us
  starting transfers between devices  411 us (73%)
  waiting for transfers between devices  79.5 us (14%)
  local copies, waits for them, and re-layouts  46.8 us (8%)
  other arithmetic  16.3 us (3%)
    ppermute x108, starting transfers between devices, passed_along(): lax.ppermute(value, axis, [(source, source + steps) for source in range(i...  371 us
    ppermute x108, waiting for transfers between devices, passed_along(): lax.ppermute(value, axis, [(source, source + steps) for source in range(i...  68 us
    ppermute x15, starting transfers between devices, partner(): return lax.ppermute(value, axis, pairs)  39.6 us
    reshape x3, local copies, waits for them, and re-layouts, coarse_faces(): blocks = beta.reshape(size_x // 2, 2, size_y // 2, 2, size_z // 2, 2)  17.4 us
    reshape x4, local copies, waits for them, and re-layouts, restrict_cells(): blocks = values.reshape(size_x // 2, 2, size_y // 2, 2, size_z // 2, 2)  12.4 us
    ppermute x15, waiting for transfers between devices, partner(): return lax.ppermute(value, axis, pairs)  11.5 us
  transfers between devices with their start and end apart: 123, of which 29 were waited for; matrix products, arithmetic and copies ran while one was open for 9% of the time, Pallas kernels for 0%

commit v1 on v0

v1 whole, which is shorter than its diff:
```python
import functools

import jax
import jax.numpy as jnp
from jax import lax
from jax.experimental import pallas as pl
from jax.experimental.pallas import tpu as pltpu
from jax.sharding import PartitionSpec as P

MESH = pl.DeviceIdType.MESH
F32 = jnp.float32
COARSE = 8

H0, H1, H2, H3 = 3, 9, 6, 10
X0, X1, X2 = 8 + 2 * H0, 4 + 2 * H1, 2 + 2 * H2
SLOTS, GROUPS = 2 * H3 + 1, (2 * H3 + 4) // 4


def reach(offset, size, halo):
    if offset == 0:
        return 0, size
    near = size * (abs(offset) - 1)
    count = min(size, halo - near)
    if count <= 0:
        return 0, 0
    return (0, count) if offset > 0 else (size - count, count)


def gap(offset, size):
    return 0 if offset == 0 else size * (abs(offset) - 1) + 1


AROUND = [(a, b) for a in (-1, 0, 1) for b in (-1, 0, 1) if (a, b) != (0, 0)]
WIDE = [
    (a, b)
    for a in range(-3, 4)
    for b in range(-3, 4)
    if (a, b) != (0, 0) and gap(a, 4) + gap(b, 4) <= H1
]
ALONG_X = [a for a in range(-H3, H3 + 1) if a]
ALONG_Y = list(range(1, 16))
NEAR = [-3, -2, -1, 1, 2, 3]
PARTNERS = sorted(set(WIDE) | {(a, 0) for a in ALONG_X} | {(0, b if b <= 8 else b - 16) for b in ALONG_Y})


def lanes(shape=(8, 128)):
    return lax.broadcasted_iota(jnp.int32, shape, 1)


def rows(shape=(8, 128)):
    return lax.broadcasted_iota(jnp.int32, shape, 0)


def pick(tile, index, axis):
    return jnp.take_along_axis(tile, index, axis=axis, mode="promise_in_bounds")


def up(value):
    return pltpu.roll(value, value.shape[0] - 1, 0)


def down(value):
    return pltpu.roll(value, 1, 0)


def right(value):
    return pltpu.roll(value, 127, 1)


def left(value):
    return pltpu.roll(value, 1, 1)


def coarsen(planes, kind, lane_index=None):
    out = []
    for i in range(0, len(planes), 2):
        total = planes[i] if kind == "x" else planes[i] + planes[i + 1]
        if kind != "y":
            total = total + up(total)
        total = pick(total, lax.rem(2 * rows(), 8), 0)
        if lane_index is not None:
            if kind != "z":
                total = total + right(total)
            total = pick(total, lane_index, 1)
        out.append(total * (0.125 if kind == "c" else 0.0625))
    return out


def couplings(get, bx, by, bz, x):
    v = get(x)
    cy, cz = by(x), bz(x)
    total = bx(x) * get(x - 1) + bx(x + 1) * get(x + 1)
    total = total + cy * down(v) + up(cy * v)
    return v, total + cz * left(v) + right(cz * v)


class Copies:
    def __init__(self, place, send_sems, recv_sems, number):
        self.place, self.number = place, number
        self.send_sem, self.recv_sem = send_sems.at[number], recv_sems.at[number]
        self.count = 0

    def start(self, source, target, offset):
        pltpu.make_async_remote_copy(
            src_ref=source,
            dst_ref=target,
            send_sem=self.send_sem,
            recv_sem=self.recv_sem,
            device_id=self.place(offset),
            device_id_type=MESH,
        ).start()
        size = 1
        for dim in source.shape:
            size *= dim
        self.count += size // 128

    def _wait(self, sem, dummy):
        part = dummy.at[pl.ds(0, self.count)]
        pltpu.make_async_copy(part, part, sem).wait()

    def arrived(self, dummy):
        self._wait(self.recv_sem, dummy)

    def sent(self, dummy):
        self._wait(self.send_sem, dummy)


def kernel(nx, ny, rhs, acoef, beta_x, beta_y, beta_z, out,
           F0, A0, E0, HX, HY, D0, W0, VA, VB, VP,
           F1, W1, P1, Q1, G1, U1,
           F2, W2, FP, P2, Q2,
           R3, RC, PK, PC, F3, W3, P3, Q3,
           dummy, send_sems, recv_sems):
    ix, iy = lax.axis_index("bx"), lax.axis_index("by")

    def place(offset):
        return (lax.rem(ix + (offset[0] % nx), nx), lax.rem(iy + (offset[1] % ny), ny))

    def group(number):
        return Copies(place, send_sems, recv_sems, number)

    barrier = pltpu.get_barrier_semaphore()
    for offset in PARTNERS:
        pl.semaphore_signal(barrier, inc=1, device_id=place(offset), device_id_type=MESH)

    lane, row = lanes(), rows()
    even = lax.rem(2 * lane, 128)
    keep_x = jnp.where(ix == 0, 0.0, 1.0).astype(F32)
    keep_y = jnp.where(iy == 0, 0.0, 1.0).astype(F32)
    keep_rows = jnp.where(row == 0, keep_y, 1.0)
    E, O = pl.ds(0, 128), pl.ds(128, 128)

    def split(ref, x):
        low, high = ref[x, :, E], ref[x, :, O]
        return tuple(
            jnp.where(lane < 64, pick(low, even + odd, 1), pick(high, even + odd, 1)) for odd in (0, 1)
        )

    own = pl.ds(0, 8)
    for x in range(8):
        px = H0 + x
        f, a, bx, by, bz = (split(ref, x) for ref in (rhs, acoef, beta_x, beta_y, beta_z))
        for half, part in ((0, E), (1, O)):
            bxm = bx[half] * keep_x if x == 0 else bx[half]
            bym = by[half] * keep_rows
            extra = by[half] - bym
            if x == 0:
                extra = extra + (bx[half] - bxm)
            bzm = bz[half]
            if half == 0:
                bzm = jnp.where(lane == 0, 0.0, bzm)
                extra = extra + (bz[half] - bzm)
            F0[0, px, own, part] = f[half]
            F0[1, px, own, part] = a[half] + extra
            F0[2, px, own, part] = bxm
            F0[3, px, own, part] = bym
            F0[4, px, own, part] = bzm
            A0[x, :, part] = a[half]
            E0[x, :, part] = extra

    pl.semaphore_wait(barrier, len(PARTNERS))

    faces = group(0)
    faces.start(F0.at[2, H0, own], HX.at[:, :], (-1, 0))
    faces.start(F0.at[3, pl.ds(H0, 8), pl.ds(0, 1)], HY.at[:, pl.ds(0, 1)], (0, -1))
    halo = group(1)

    def span_x(offset, wide):
        if offset == 0:
            return pl.ds(H0, 8), pl.ds(H0, 8)
        if offset < 0:
            return pl.ds(H0, wide), pl.ds(H0 + 8, wide)
        return pl.ds(H0 + 8 - wide, wide), pl.ds(H0 - wide, wide)

    def span_y(offset, wide):
        if offset == 0:
            return pl.ds(0, 8), pl.ds(0, 8)
        if offset < 0:
            return pl.ds(0, wide), pl.ds(8, wide)
        return pl.ds(8 - wide, wide), pl.ds(16 - wide, wide)

    def spans(dx, dy):
        width = 2 if dx > 0 and dy > 0 else 3
        sx, tx = span_x(dx, width)
        sy, ty = span_y(dy, width)
        return sx, sy, tx, ty

    for dx, dy in AROUND:
        sx, sy, tx, ty = spans(dx, dy)
        halo.start(F0.at[:, sx, sy], F0.at[:, tx, ty], (dx, dy))
    halo.start(F0.at[2, H0 + 3, own], F0.at[2, H0 + 11, own], (-1, 0))
    halo.start(F0.at[3, pl.ds(H0, 8), pl.ds(3, 1)], F0.at[3, pl.ds(H0, 8), pl.ds(11, 1)], (0, -1))

    def both(get):
        return [get(x, E) + get(x, O) for x in range(8)]

    to64, to32 = even, lax.rem(2 * lane, 64)
    a1 = coarsen(both(lambda x, p: A0[x, :, p]), "c")
    e1 = [0.5 * t for t in coarsen(both(lambda x, p: E0[x, :, p]), "c")]
    bx1 = coarsen(both(lambda x, p: F0[2, H0 + x, own, p]), "x")
    by1 = coarsen(both(lambda x, p: F0[3, H0 + x, own, p]), "y")
    bz1 = coarsen([F0[4, H0 + x, own, E] for x in range(8)], "z")
    a2 = coarsen(a1, "c", to64)
    e2 = [0.5 * t for t in coarsen(e1, "c", to64)]
    bx2, by2, bz2 = coarsen(bx1, "x", to64), coarsen(by1, "y", to64), coarsen(bz1, "z", to64)
    a3 = coarsen(a2, "c", to32)
    e3 = [0.5 * t for t in coarsen(e2, "c", to32)]
    bx3, by3, bz3 = coarsen(bx2, "x", to32), coarsen(by2, "y", to32), coarsen(bz2, "z", to32)

    faces.arrived(dummy)
    hx = HX[:, E] + HX[:, O]
    hx1 = coarsen([hx, hx], "x")[0]
    hx2 = coarsen([hx1, hx1], "x", to64)[0]
    hx3 = coarsen([hx2, hx2], "x", to32)[0]
    hy = [HY[x, :, E] + HY[x, :, O] for x in range(8)]
    hy1 = [0.0625 * (hy[2 * i] + hy[2 * i + 1]) for i in range(4)]

    def squeeze(t, index):
        return pick(t + right(t), index, 1) * 0.0625

    hy2 = [squeeze(hy1[2 * i] + hy1[2 * i + 1], to64) for i in range(2)]
    hy3 = squeeze(hy2[0] + hy2[1], to32)

    def diag_of(a, e, bx, by, bz, hx_plane, hy_rows, last):
        result = []
        for i in range(len(a)):
            high_x = bx[i + 1] if i + 1 < len(a) else hx_plane
            edge = pltpu.roll(hy_rows[i], last, 0) if last else hy_rows[i]
            high_y = jnp.where(row == last, edge, up(by[i]))
            result.append(a[i] + e[i] + bx[i] + high_x + by[i] + high_y + bz[i] + right(bz[i]))
        return result

    d1 = diag_of(a1, e1, bx1, by1, bz1, hx1, hy1, 3)
    d2 = diag_of(a2, e2, bx2, by2, bz2, hx2, hy2, 1)
    d3 = diag_of(a3, e3, bx3, by3, bz3, hx3, [hy3], 0)
    for number, field in enumerate((d1, bx1, by1, bz1)):
        for i in range(4):
            F1[1 + number, H1 + i, pl.ds(0, 4)] = field[i][0:4]
    for number, field in enumerate((d2, bx2, by2, bz2)):
        for i in range(2):
            F2[2 + number, H2 + i, pl.ds(0, 2)] = field[i][0:2]
    for number, field in enumerate((d3, bx3, by3, bz3)):
        RC[number, H3] = field[0][0:1]

    def wide_spans(dx, dy):
        fx, cx = reach(-dx, 4, H1)
        fy, cy = reach(-dy, 4, H1)
        return pl.ds(H1 + fx, cx), pl.ds(fy, cy), pl.ds(H1 - 4 * dx + fx, cx), pl.ds((fy - 4 * dy) % 24, cy)

    wide = group(2)
    for dx, dy in WIDE:
        sx, sy, tx, ty = wide_spans(dx, dy)
        wide.start(F1.at[pl.ds(1, 4), sx, sy], F1.at[pl.ds(1, 4), tx, ty], (dx, dy))
    two = pl.ds(0, 2)
    mid = pl.ds(H2, 2)
    coef2x = group(3)
    for dx in NEAR:
        coef2x.start(F2.at[pl.ds(2, 4), mid, two], F2.at[pl.ds(2, 4), pl.ds(H2 - 2 * dx, 2), two], (dx, 0))
    coef3x = group(4)
    for dx in ALONG_X:
        coef3x.start(RC.at[:, H3], RC.at[:, H3 - dx], (dx, 0))

    halo.arrived(dummy)
    for x in range(X0):
        hz = F0[4, x, :, E], F0[4, x, :, O]
        for half, part in ((0, E), (1, O)):
            by = F0[3, x, :, part]
            total = F0[1, x, :, part] + F0[2, x, :, part] + F0[2, x + 1, :, part] + by + up(by) + hz[half]
            total = total + (hz[1] if half == 0 else right(hz[0]))
            w = 0.8 / total
            W0[x, :, part] = w
            VA[x, :, part] = w * F0[0, x, :, part]
            if H0 <= x < H0 + 8:
                D0[x - H0, :, part] = total[0:8]

    def couplings0(src, x, count=16):
        ve, vo = src[x, :, E], src[x, :, O]
        ze, zo = F0[4, x, :, E], F0[4, x, :, O]
        sums = []
        for v, part in ((ve, E), (vo, O)):
            by = F0[3, x, :, part]
            total = F0[2, x, :, part] * src[x - 1, :, part] + F0[2, x + 1, :, part] * src[x + 1, :, part]
            sums.append(total + by * down(v) + up(by * v))
        sums[0] = sums[0] + ze * left(vo) + zo * vo
        sums[1] = sums[1] + zo * ve + right(ze * ve)
        return ((ve, sums[0], E), (vo, sums[1], O))

    def sweep0(src, dst, first, last):
        for x in range(first, last):
            for v, total, part in couplings0(src, x):
                dst[x, :, part] = 0.2 * v + W0[x, :, part] * (F0[0, x, :, part] + total)

    sweep0(VA, VB, 1, X0 - 1)
    sweep0(VB, VA, 2, X0 - 2)
    remains = []
    for x in range(8):
        parts = []
        for v, total, part in couplings0(VA, H0 + x):
            v, total = v[0:8], total[0:8]
            parts.append(F0[0, H0 + x, own, part] + total - D0[x, :, part] * v)
            VP[H0 + x, own, part] = v
        remains.append(parts[0] + parts[1])
    f1 = coarsen(remains, "c")
    for i in range(4):
        F1[0, H1 + i, pl.ds(0, 4)] = f1[i][0:4]

    wide_f = group(5)
    for dx, dy in WIDE:
        sx, sy, tx, ty = wide_spans(dx, dy)
        wide_f.start(F1.at[0, sx, sy], F1.at[0, tx, ty], (dx, dy))
    halo_v = group(6)
    for dx, dy in AROUND:
        sx, sy, tx, ty = spans(dx, dy)
        halo_v.start(VP.at[sx, sy], VP.at[tx, ty], (dx, dy))

    every = pl.ds(0, X2)
    coef2x.arrived(dummy)
    coef2y = group(7)
    for dy in NEAR:
        target = pl.ds((-2 * dy) % 16, 2)
        coef2y.start(F2.at[pl.ds(2, 4), every, two], F2.at[pl.ds(2, 4), every, target], (0, dy))

    def packed(get):
        result = []
        for g in range(GROUPS):
            columns = [get(min(4 * g + k, SLOTS - 1)) for k in range(4)]
            line = lane[0:1]
            result.append(
                jnp.where(
                    line < 64,
                    jnp.where(line < 32, columns[0], columns[1]),
                    jnp.where(line < 96, columns[2], columns[3]),
                )
            )
        return result

    one = pl.ds(0, 1)
    coef3x.arrived(dummy)
    for number in range(4):
        for g, value in enumerate(packed(lambda s: RC[number, s])):
            PC[number, g, one] = value
            F3[1 + number, g, one] = value
    coef3y = group(8)
    for dy in ALONG_Y:
        coef3y.start(PC.at[:, :, one], F3.at[pl.ds(1, 4), :, pl.ds(16 - dy, 1)], (0, dy))

    wide.arrived(dummy)
    for x in range(X1):
        W1[x] = 0.8 / F1[1, x]
    coef2y.arrived(dummy)
    for x in range(X2):
        W2[x] = 0.8 / F2[2, x]

    def face(ref, number):
        return lambda x: ref[number, x]

    def sweep(src, dst, coeffs, source, weight, first, last, shift=0):
        for x in range(first, last):
            v, total = couplings(lambda p: src[p - shift], *coeffs, x)
            dst[x - shift] = 0.2 * v + weight[x] * (source(x) + total)

    c1 = face(F1, 2), face(F1, 3), face(F1, 4)
    wide_f.arrived(dummy)
    for x in range(X1):
        P1[x] = W1[x] * F1[0, x]
    sweep(P1, Q1, c1, face(F1, 0), W1, 1, X1 - 1)
    sweep(Q1, P1, c1, face(F1, 0), W1, 2, X1 - 2)

    def remains1(x):
        v, total = couplings(lambda p: P1[p], *c1, x)
        return F1[0, x] + total - F1[1, x] * v

    pairs = lax.rem(2 * row, 8)
    for i in range(8):
        x = H1 - 6 + 2 * i
        total = remains1(x) + remains1(x + 1)
        tiles = []
        for t in range(3):
            tile = total[8 * t : 8 * t + 8]
            tiles.append(pick(tile + up(tile), pairs, 0))
        tiles = [jnp.where(row < 4, tiles[0], tiles[1]), tiles[2]]
        tiles = [pick(tile + right(tile), to64, 1) * 0.125 for tile in tiles]
        FP[i] = jnp.concatenate(tiles, axis=0)

    c2 = face(F2, 3), face(F2, 4), face(F2, 5)
    for i in range(8):
        P2[i] = W2[i + 3] * FP[i]
    sweep(P2, Q2, c2, lambda x: FP[x - 3], W2, 4, 10, 3)
    sweep(Q2, P2, c2, lambda x: FP[x - 3], W2, 5, 9, 3)
    total = None
    for x in (6, 7):
        v, s = couplings(lambda p: P2[p - 3], *c2, x)
        rest = (FP[x - 3] + s - F2[2, x] * v)[0:8]
        total = rest if total is None else total + rest
        F2[0, x, two] = FP[x - 3][0:2]
        F2[1, x, two] = v[0:2]
    total = total + up(total)
    f3 = (pick(total + right(total), to32, 1) * 0.125)[0:1]
    R3[H3] = f3

    near3x = group(9)
    for dx in ALONG_X:
        near3x.start(R3.at[H3], R3.at[H3 - dx], (dx, 0))
    near2x = group(10)
    for dx in NEAR:
        near2x.start(F2.at[two, mid, two], F2.at[two, pl.ds(H2 - 2 * dx, 2), two], (dx, 0))

    for x in range(14):
        p = H1 - 5 + x
        for number, get in enumerate((face(F1, 0), lambda q: W1[q], face(F1, 2), face(F1, 3), face(F1, 4), lambda q: P1[q])):
            value = get(p)
            mixed = jnp.where(row < 3, value[8:16], value[16:24])
            G1[number, x] = jnp.concatenate([value[0:8], mixed], axis=0)
    coef3y.arrived(dummy)
    for g in range(GROUPS):
        W3[g] = 0.8 / F3[1, g]

    near3x.arrived(dummy)
    for g, value in enumerate(packed(lambda s: R3[s])):
        PK[g, one] = value
        F3[0, g, one] = value
    near3y = group(11)
    for dy in ALONG_Y:
        near3y.start(PK.at[:, one], F3.at[0, :, pl.ds(16 - dy, 1)], (0, dy))
    near2x.arrived(dummy)
    near2y = group(12)
    for dy in NEAR:
        target = pl.ds((-2 * dy) % 16, 2)
        near2y.start(F2.at[two, every, two], F2.at[two, every, target], (0, dy))
    halo_v.arrived(dummy)
    faces.sent(dummy)
    halo.sent(dummy)
    wide.sent(dummy)
    coef2x.sent(dummy)
    coef3x.sent(dummy)
    wide_f.sent(dummy)
    halo_v.sent(dummy)
    coef2y.sent(dummy)
    coef3y.sent(dummy)
    near3x.sent(dummy)
    near2x.sent(dummy)

    near3y.arrived(dummy)
    line = lanes((16, 128))
    for g in range(GROUPS):
        P3[g] = W3[g] * F3[0, g]
    src, dst = P3, Q3
    for step in range(COARSE - 1):
        for g in range(GROUPS):
            v, cx, cy, cz = src[g], F3[2, g], F3[3, g], F3[4, g]
            ahead = min(g + 1, GROUPS - 1)
            low = jnp.where(line < 32, pltpu.roll(src[max(g - 1, 0)], 32, 1), pltpu.roll(v, 32, 1))
            high = jnp.where(
                line >= 96, pltpu.roll(F3[2, ahead] * src[ahead], 96, 1), pltpu.roll(cx * v, 96, 1)
            )
            total = cx * low + high + cy * down(v) + up(cy * v) + cz * left(v) + right(cz * v)
            dst[g] = 0.2 * v + W3[g] * (F3[0, g] + total)
        src, dst = dst, src

    half_rows = lax.shift_right_logical(row, 1)

    def onto2(x):
        slot = H3 + x
        index = 32 * (slot % 4) + lax.shift_right_logical(lax.rem(lane, 64), 1)
        value = src[slot // 4]
        low, high = (pick(value[8 * t : 8 * t + 8], index, 1) for t in (0, 1))
        return jnp.concatenate([pick(low, half_rows, 0), pick(high, half_rows + 4, 0)], axis=0)

    lifted = [onto2(x) for x in range(-3, 4)]
    near2y.arrived(dummy)
    for x in range(X2):
        P2[x] = F2[1, x] + lifted[x // 2]
    sweep(P2, Q2, c2, face(F2, 0), W2, 1, X2 - 1)
    sweep(Q2, P2, c2, face(F2, 0), W2, 2, X2 - 2)
    sweep(P2, Q2, c2, face(F2, 0), W2, 3, X2 - 3)

    half_lanes = lax.shift_right_logical(lane, 1)

    def finer(value, limit, lane_index=None):
        tiles = [value[0:8], value[8:16]]
        if lane_index is not None:
            tiles = [pick(tile, lane_index, 1) for tile in tiles]
        upper = jnp.where(row < limit, pick(tiles[0], half_rows + 4, 0), pick(tiles[1], half_rows + 4, 0))
        return jnp.concatenate([pick(tiles[0], half_rows, 0), upper], axis=0)

    lifted = [finer(Q2[H2 + x], 3, half_lanes) for x in range(-3, 5)]
    for x in range(14):
        P1_16 = G1[5, x] + lifted[(x - 5) // 2 + 3]
        U1[0, x] = P1_16
    g1 = face(G1, 2), face(G1, 3), face(G1, 4)
    even_v, odd_v = U1.at[0], U1.at[1]
    weight1 = G1.at[1]
    sweep(even_v, odd_v, g1, face(G1, 0), weight1, 1, 13)
    sweep(odd_v, even_v, g1, face(G1, 0), weight1, 2, 12)
    sweep(even_v, odd_v, g1, face(G1, 0), weight1, 3, 11)

    lifted = [finer(odd_v[5 + x], 4) for x in range(-2, 6)]
    for x in range(X0):
        for part in (E, O):
            VA[x, :, part] = VP[x, :, part] + lifted[(x - 3) // 2 + 2]
    sweep0(VA, VB, 1, X0 - 1)
    sweep0(VB, VA, 2, X0 - 2)
    is_even = lax.rem(lane, 2) == 0
    for x in range(8):
        halves = []
        for v, total, part in couplings0(VA, H0 + x):
            result = 0.2 * v[0:8] + W0[H0 + x, own, part] * (F0[0, H0 + x, own, part] + total[0:8])
            halves.append(result)
        for part, index in ((E, half_lanes), (O, half_lanes + 64)):
            out[x, :, part] = jnp.where(is_even, pick(halves[0], index, 1), pick(halves[1], index, 1))

    near3y.sent(dummy)
    near2y.sent(dummy)


def solution(mesh):
    nx, ny = mesh.shape["bx"], mesh.shape["by"]

    def vmem(*shape):
        return pltpu.VMEM(shape, F32)

    def body(*args):
        return pl.pallas_call(
            functools.partial(kernel, nx, ny),
            out_shape=jax.ShapeDtypeStruct((8, 8, 256), F32),
            in_specs=[pl.BlockSpec(memory_space=pltpu.VMEM)] * 5,
            out_specs=pl.BlockSpec(memory_space=pltpu.VMEM),
            scratch_shapes=[
                vmem(5, X0 + 1, 16, 256), vmem(8, 8, 256), vmem(8, 8, 256), vmem(8, 256), vmem(8, 8, 256),
                vmem(8, 8, 256), vmem(X0, 16, 256), vmem(X0, 16, 256), vmem(X0, 16, 256), vmem(X0, 16, 256),
                vmem(5, X1 + 1, 24, 128), vmem(X1, 24, 128), vmem(X1, 24, 128), vmem(X1, 24, 128),
                vmem(6, 14, 16, 128), vmem(2, 14, 16, 128),
                vmem(6, X2, 16, 128), vmem(X2, 16, 128), vmem(8, 16, 128), vmem(X2, 16, 128), vmem(X2, 16, 128),
                vmem(SLOTS, 1, 128), vmem(4, SLOTS, 1, 128), vmem(GROUPS, 8, 128), vmem(4, GROUPS, 8, 128),
                vmem(5, GROUPS, 16, 128), vmem(GROUPS, 16, 128), vmem(GROUPS, 16, 128), vmem(GROUPS, 16, 128),
                vmem(8192, 128),
                pltpu.SemaphoreType.DMA((13,)), pltpu.SemaphoreType.DMA((13,)),
            ],
            compiler_params=pltpu.CompilerParams(
                collective_id=0, has_side_effects=True, vmem_limit_bytes=40 * 2**20
            ),
        )(*args)

    return jax.shard_map(
        body,
        mesh=mesh,
        in_specs=(P("bx", "by", None),) * 5,
        out_specs=P("bx", "by", None),
        check_vma=False,
    )
```

time: 560 us -> 58.7 us (0.10)
  the two profiles are of different devices: /device:TPU:398 before, /device:TPU:1 now
where the time goes in v1:
time: 58.7 us; the launch traced here: 57.7 us
  Pallas kernels  52.9 us (90%)
  local copies, waits for them, and re-layouts  4.83 us (8%)
    pallas_call x1, Pallas kernels, body(): pl.pallas_call(functools.partial(kernel, nx, ny), out_shape=jax.ShapeDtyp...  52.9 us
    unnamed x11, local copies, waits for them, and re-layouts  4.83 us

profile of v1, /device:TPU:1, one launch (start us, length us, event | category | flops | bytes accessed | tf_op | source)
XLA Modules:
  0.0 57.7 jit_solution(14863346726243112369)
XLA Ops:
  0.0 0.0 copy-start
  0.0 0.8 %copy-done = f32[8,8,256]{2,1,0:T(8,128)S(1)} copy-done((f32[8,8,256]{2,1,0:T(8,128)S(1)}, f32[8,8,256]{2,1,0:T(8,128)}, u32[]{:S(2)}) %copy-start) | copy-done | bytes 65560
  0.8 0.0 copy-start.1
  0.8 0.8 %copy-done.1 = f32[8,8,256]{2,1,0:T(8,128)S(1)} copy-done((f32[8,8,256]{2,1,0:T(8,128)S(1)}, f32[8,8,256]{2,1,0:T(8,128)}, u32[]{:S(2)}) %copy-start.1) | copy-done | bytes 65560
  1.7 0.0 copy-start.2
  1.7 0.8 %copy-done.2 = f32[8,8,256]{2,1,0:T(8,128)S(1)} copy-done((f32[8,8,256]{2,1,0:T(8,128)S(1)}, f32[8,8,256]{2,1,0:T(8,128)}, u32[]{:S(2)}) %copy-start.2) | copy-done | bytes 65560
  2.5 0.0 copy-start.3
  2.5 0.8 %copy-done.3 = f32[8,8,256]{2,1,0:T(8,128)S(1)} copy-done((f32[8,8,256]{2,1,0:T(8,128)S(1)}, f32[8,8,256]{2,1,0:T(8,128)}, u32[]{:S(2)}) %copy-start.3) | copy-done | bytes 65560
  3.4 0.0 copy-start.4
  3.4 0.8 %copy-done.4 = f32[8,8,256]{2,1,0:T(8,128)S(1)} copy-done((f32[8,8,256]{2,1,0:T(8,128)S(1)}, f32[8,8,256]{2,1,0:T(8,128)}, u32[]{:S(2)}) %copy-start.4) | copy-done | bytes 65560
  4.2 52.9 %shard_map.55 = f32[8,8,256]{2,1,0:T(8,128)S(1)} custom-call(f32[8,8,256]{2,1,0:T(8,128)S(1)} %copy-done, f32[8,8,256]{2,1,0:T(8,128)S(1)} %copy-done.1, f32[8,8,256]{2,1,0:T(8,128)S(1)} %copy-done.2, f32[8,8,256]{2,1,0:T(8,128)S(1)} %copy-done.3, f32[8,8,256]{2,1,0:T(8,128)S(1)} %copy-done.4), custom_call_target="tpu_custom_call" | custom-call | tf_op jit(solution)/shard_map/pallas_call | solution.py:543
  57.1 0.6 %copy.7 = f32[8,8,256]{2,1,0:T(8,128)} copy(f32[8,8,256]{2,1,0:T(8,128)S(1)} %shard_map.55) | data formatting | bytes 131072
Async XLA Ops:
  0.0 0.8 %copy-start = (f32[8,8,256]{2,1,0:T(8,128)S(1)}, f32[8,8,256]{2,1,0:T(8,128)}, u32[]{:S(2)}) copy-start(f32[8,8,256]{2,1,0:T(8,128)} %rhs.1) | copy-start | bytes 196612
  0.8 0.8 %copy-start.1 = (f32[8,8,256]{2,1,0:T(8,128)S(1)}, f32[8,8,256]{2,1,0:T(8,128)}, u32[]{:S(2)}) copy-start(f32[8,8,256]{2,1,0:T(8,128)} %acoef.1) | copy-start | bytes 196612
  1.7 0.8 %copy-start.2 = (f32[8,8,256]{2,1,0:T(8,128)S(1)}, f32[8,8,256]{2,1,0:T(8,128)}, u32[]{:S(2)}) copy-start(f32[8,8,256]{2,1,0:T(8,128)} %beta_x.1) | copy-start | bytes 196612
  2.5 0.8 %copy-start.3 = (f32[8,8,256]{2,1,0:T(8,128)S(1)}, f32[8,8,256]{2,1,0:T(8,128)}, u32[]{:S(2)}) copy-start(f32[8,8,256]{2,1,0:T(8,128)} %beta_y.1) | copy-start | bytes 196612
  3.4 0.8 %copy-start.4 = (f32[8,8,256]{2,1,0:T(8,128)S(1)}, f32[8,8,256]{2,1,0:T(8,128)}, u32[]{:S(2)}) copy-start(f32[8,8,256]{2,1,0:T(8,128)} %beta_z.1) | copy-start | bytes 196612

commit v2 on v1

--- a/solution.py
+++ b/solution.py
@@ -126,12 +126,18 @@
 
 
 def kernel(nx, ny, rhs, acoef, beta_x, beta_y, beta_z, out,
-           F0, A0, E0, HX, HY, D0, W0, VA, VB, VP,
+           IN, in_sems, F0, A0, E0, HX, HY, D0, W0, VA, VB, VP,
            F1, W1, P1, Q1, G1, U1,
-           F2, W2, FP, P2, Q2,
+           F2, S2, T2, W2, FP, P2, Q2,
            R3, RC, PK, PC, F3, W3, P3, Q3,
            dummy, send_sems, recv_sems):
     ix, iy = lax.axis_index("bx"), lax.axis_index("by")
+    loads = [
+        pltpu.make_async_copy(ref, IN.at[number], in_sems.at[number])
+        for number, ref in enumerate((beta_x, beta_y, beta_z, acoef, rhs))
+    ]
+    for load in loads:
+        load.start()
 
     def place(offset):
         return (lax.rem(ix + (offset[0] % nx), nx), lax.rem(iy + (offset[1] % ny), ny))
@@ -150,16 +156,18 @@
     keep_rows = jnp.where(row == 0, keep_y, 1.0)
     E, O = pl.ds(0, 128), pl.ds(128, 128)
 
-    def split(ref, x):
-        low, high = ref[x, :, E], ref[x, :, O]
+    def split(number, x):
+        low, high = IN[number, x, :, E], IN[number, x, :, O]
         return tuple(
             jnp.where(lane < 64, pick(low, even + odd, 1), pick(high, even + odd, 1)) for odd in (0, 1)
         )
 
     own = pl.ds(0, 8)
+    for load in loads:
+        load.wait()
     for x in range(8):
         px = H0 + x
-        f, a, bx, by, bz = (split(ref, x) for ref in (rhs, acoef, beta_x, beta_y, beta_z))
+        bx, by, bz, a, f = (split(number, x) for number in range(5))
         for half, part in ((0, E), (1, O)):
             bxm = bx[half] * keep_x if x == 0 else bx[half]
             bym = by[half] * keep_rows
@@ -200,7 +208,7 @@
         return pl.ds(8 - wide, wide), pl.ds(16 - wide, wide)
 
     def spans(dx, dy):
-        width = 2 if dx > 0 and dy > 0 else 3
+        width = 2 if dx != 0 and dy != 0 else 3
         sx, tx = span_x(dx, width)
         sy, ty = span_y(dy, width)
         return sx, sy, tx, ty
@@ -210,6 +218,12 @@
         halo.start(F0.at[:, sx, sy], F0.at[:, tx, ty], (dx, dy))
     halo.start(F0.at[2, H0 + 3, own], F0.at[2, H0 + 11, own], (-1, 0))
     halo.start(F0.at[3, pl.ds(H0, 8), pl.ds(3, 1)], F0.at[3, pl.ds(H0, 8), pl.ds(11, 1)], (0, -1))
+    for dx, dy, number, x, y in (
+        (-1, -1, 2, 2, 0), (-1, -1, 3, 2, 0), (-1, -1, 2, 0, 2), (-1, -1, 3, 0, 2),
+        (-1, 1, 2, 2, 7), (-1, 1, 2, 0, 5), (1, -1, 3, 7, 2), (1, -1, 3, 5, 0),
+    ):
+        source = F0.at[number, H0 + x, pl.ds(y, 1)]
+        halo.start(source, F0.at[number, H0 + x - 8 * dx, pl.ds((y - 8 * dy) % 16, 1)], (dx, dy))
 
     def both(get):
         return [get(x, E) + get(x, O) for x in range(8)]
@@ -227,6 +241,23 @@
     e3 = [0.5 * t for t in coarsen(e2, "c", to32)]
     bx3, by3, bz3 = coarsen(bx2, "x", to32), coarsen(by2, "y", to32), coarsen(bz2, "z", to32)
 
+    for number, field in enumerate((bx1, by1, bz1)):
+        for i in range(4):
+            F1[2 + number, H1 + i, pl.ds(0, 4)] = field[i][0:4]
+
+    def wide_spans(dx, dy):
+        fx, cx = reach(-dx, 4, H1)
+        fy, cy = reach(-dy, 4, H1)
+        return pl.ds(H1 + fx, cx), pl.ds(fy, cy), pl.ds(H1 - 4 * dx + fx, cx), pl.ds((fy - 4 * dy) % 24, cy)
+
+    def send1(numbers, offset, collection):
+        sx, sy, tx, ty = wide_spans(*offset)
+        collection.start(F1.at[numbers, sx, sy], F1.at[numbers, tx, ty], offset)
+
+    faces1y = group(2)
+    for dy in NEAR:
+        send1(pl.ds(2, 3), (0, dy), faces1y)
+
     faces.arrived(dummy)
     hx = HX[:, E] + HX[:, O]
     hx1 = coarsen([hx, hx], "x")[0]
@@ -253,30 +284,27 @@
     d1 = diag_of(a1, e1, bx1, by1, bz1, hx1, hy1, 3)
     d2 = diag_of(a2, e2, bx2, by2, bz2, hx2, hy2, 1)
     d3 = diag_of(a3, e3, bx3, by3, bz3, hx3, [hy3], 0)
-    for number, field in enumerate((d1, bx1, by1, bz1)):
-        for i in range(4):
-            F1[1 + number, H1 + i, pl.ds(0, 4)] = field[i][0:4]
-    for number, field in enumerate((d2, bx2, by2, bz2)):
-        for i in range(2):
-            F2[2 + number, H2 + i, pl.ds(0, 2)] = field[i][0:2]
+    for i in range(4):
+        F1[1, H1 + i, pl.ds(0, 4)] = d1[i][0:4]
+    two = pl.ds(0, 2)
+    mid = pl.ds(H2, 2)
+    for i in range(2):
+        own2 = [jnp.where(lane < 64, a, b) for a, b in ((d2[i], bx2[i]), (by2[i], bz2[i]))]
+        for number in range(2):
+            S2[number, H2 + i, two] = own2[number][0:2]
     for number, field in enumerate((d3, bx3, by3, bz3)):
         RC[number, H3] = field[0][0:1]
 
-    def wide_spans(dx, dy):
-        fx, cx = reach(-dx, 4, H1)
-        fy, cy = reach(-dy, 4, H1)
-        return pl.ds(H1 + fx, cx), pl.ds(fy, cy), pl.ds(H1 - 4 * dx + fx, cx), pl.ds((fy - 4 * dy) % 24, cy)
-
-    wide = group(2)
-    for dx, dy in WIDE:
-        sx, sy, tx, ty = wide_spans(dx, dy)
-        wide.start(F1.at[pl.ds(1, 4), sx, sy], F1.at[pl.ds(1, 4), tx, ty], (dx, dy))
-    two = pl.ds(0, 2)
-    mid = pl.ds(H2, 2)
-    coef2x = group(3)
+    diag1y = group(3)
+    for dy in NEAR:
+        send1(pl.ds(1, 1), (0, dy), diag1y)
+    coef1x = group(4)
     for dx in NEAR:
-        coef2x.start(F2.at[pl.ds(2, 4), mid, two], F2.at[pl.ds(2, 4), pl.ds(H2 - 2 * dx, 2), two], (dx, 0))
-    coef3x = group(4)
+        send1(pl.ds(1, 4), (dx, 0), coef1x)
+    coef2y = group(6)
+    for dy in NEAR:
+        coef2y.start(S2.at[:, mid, two], S2.at[:, mid, pl.ds((-2 * dy) % 16, 2)], (0, dy))
+    coef3x = group(8)
     for dx in ALONG_X:
         coef3x.start(RC.at[:, H3], RC.at[:, H3 - dx], (dx, 0))
 
@@ -324,21 +352,33 @@
     for i in range(4):
         F1[0, H1 + i, pl.ds(0, 4)] = f1[i][0:4]
 
-    wide_f = group(5)
-    for dx, dy in WIDE:
-        sx, sy, tx, ty = wide_spans(dx, dy)
-        wide_f.start(F1.at[0, sx, sy], F1.at[0, tx, ty], (dx, dy))
-    halo_v = group(6)
-    for dx, dy in AROUND:
-        sx, sy, tx, ty = spans(dx, dy)
-        halo_v.start(VP.at[sx, sy], VP.at[tx, ty], (dx, dy))
-
-    every = pl.ds(0, X2)
-    coef2x.arrived(dummy)
-    coef2y = group(7)
-    for dy in NEAR:
-        target = pl.ds((-2 * dy) % 16, 2)
-        coef2y.start(F2.at[pl.ds(2, 4), every, two], F2.at[pl.ds(2, 4), every, target], (0, dy))
+    wide_f = group(9)
+    for offset in WIDE:
+        sx, sy, tx, ty = wide_spans(*offset)
+        wide_f.start(F1.at[0, sx, sy], F1.at[0, tx, ty], offset)
+
+    faces1y.arrived(dummy)
+    diag1y.arrived(dummy)
+    corner1x = group(5)
+    for dx in (-2, -1, 1, 2):
+        fx, cx = reach(-dx, 4, H1)
+        for first, count in ((4, 4), (20, 4)) if abs(dx) == 2 else ((4, 4), (8, 4), (16, 8)):
+            span = pl.ds(first, count)
+            corner1x.start(
+                F1.at[pl.ds(1, 4), pl.ds(H1 + fx, cx), span],
+                F1.at[pl.ds(1, 4), pl.ds(H1 - 4 * dx + fx, cx), span],
+                (dx, 0),
+            )
+
+    def along_x2(collection, ref, lead):
+        for dx in NEAR:
+            for first, count in {1: ((0, 8), (10, 6)), 2: ((0, 5), (13, 3)), 3: ((0, 3), (15, 1))}[abs(dx)]:
+                source = ref.at[(*lead, mid, pl.ds(first, count))]
+                collection.start(source, ref.at[(*lead, pl.ds(H2 - 2 * dx, 2), pl.ds(first, count))], (dx, 0))
+
+    coef2y.arrived(dummy)
+    coef2x = group(7)
+    along_x2(coef2x, S2, (slice(None),))
 
     def packed(get):
         result = []
@@ -360,15 +400,20 @@
         for g, value in enumerate(packed(lambda s: RC[number, s])):
             PC[number, g, one] = value
             F3[1 + number, g, one] = value
-    coef3y = group(8)
-    for dy in ALONG_Y:
-        coef3y.start(PC.at[:, :, one], F3.at[pl.ds(1, 4), :, pl.ds(16 - dy, 1)], (0, dy))
-
-    wide.arrived(dummy)
+    coef1x.arrived(dummy)
+    corner1x.arrived(dummy)
     for x in range(X1):
         W1[x] = 0.8 / F1[1, x]
-    coef2y.arrived(dummy)
+    coef2x.arrived(dummy)
+    wide_lanes = lanes((16, 128))
+
+    def unpacked(value):
+        swapped = pltpu.roll(value, 64, 1)
+        return jnp.where(wide_lanes < 64, value, swapped), jnp.where(wide_lanes < 64, swapped, value)
+
     for x in range(X2):
+        F2[2, x], F2[3, x] = unpacked(S2[0, x])
+        F2[4, x], F2[5, x] = unpacked(S2[1, x])
         W2[x] = 0.8 / F2[2, x]
 
     def face(ref, number):
@@ -412,18 +457,24 @@
         v, s = couplings(lambda p: P2[p - 3], *c2, x)
         rest = (FP[x - 3] + s - F2[2, x] * v)[0:8]
         total = rest if total is None else total + rest
-        F2[0, x, two] = FP[x - 3][0:2]
-        F2[1, x, two] = v[0:2]
+        T2[x, two] = jnp.where(lane < 64, FP[x - 3][0:8], v[0:8])[0:2]
     total = total + up(total)
     f3 = (pick(total + right(total), to32, 1) * 0.125)[0:1]
     R3[H3] = f3
 
-    near3x = group(9)
+    near3x = group(10)
     for dx in ALONG_X:
         near3x.start(R3.at[H3], R3.at[H3 - dx], (dx, 0))
-    near2x = group(10)
-    for dx in NEAR:
-        near2x.start(F2.at[two, mid, two], F2.at[two, pl.ds(H2 - 2 * dx, 2), two], (dx, 0))
+    near2y = group(11)
+    for dy in NEAR:
+        near2y.start(T2.at[mid, two], T2.at[mid, pl.ds((-2 * dy) % 16, 2)], (0, dy))
+    coef3y = group(13)
+    for dy in ALONG_Y:
+        coef3y.start(PC.at[:, :, one], F3.at[pl.ds(1, 4), :, pl.ds(16 - dy, 1)], (0, dy))
+    halo_v = group(12)
+    for dx, dy in AROUND:
+        sx, sy, tx, ty = spans(dx, dy)
+        halo_v.start(VP.at[sx, sy], VP.at[tx, ty], (dx, dy))
 
     for x in range(14):
         p = H1 - 5 + x
@@ -431,34 +482,22 @@
             value = get(p)
             mixed = jnp.where(row < 3, value[8:16], value[16:24])
             G1[number, x] = jnp.concatenate([value[0:8], mixed], axis=0)
-    coef3y.arrived(dummy)
-    for g in range(GROUPS):
-        W3[g] = 0.8 / F3[1, g]
-
     near3x.arrived(dummy)
     for g, value in enumerate(packed(lambda s: R3[s])):
         PK[g, one] = value
         F3[0, g, one] = value
-    near3y = group(11)
+    near3y = group(14)
     for dy in ALONG_Y:
         near3y.start(PK.at[:, one], F3.at[0, :, pl.ds(16 - dy, 1)], (0, dy))
-    near2x.arrived(dummy)
-    near2y = group(12)
-    for dy in NEAR:
-        target = pl.ds((-2 * dy) % 16, 2)
-        near2y.start(F2.at[two, every, two], F2.at[two, every, target], (0, dy))
+    near2y.arrived(dummy)
+    near2x = group(15)
+    along_x2(near2x, T2, ())
+    coef3y.arrived(dummy)
+    for g in range(GROUPS):
+        W3[g] = 0.8 / F3[1, g]
     halo_v.arrived(dummy)
-    faces.sent(dummy)
-    halo.sent(dummy)
-    wide.sent(dummy)
-    coef2x.sent(dummy)
-    coef3x.sent(dummy)
-    wide_f.sent(dummy)
-    halo_v.sent(dummy)
-    coef2y.sent(dummy)
-    coef3y.sent(dummy)
-    near3x.sent(dummy)
-    near2x.sent(dummy)
+    for done in (faces, halo, faces1y, diag1y, coef1x, coef2y, coef3x, wide_f, corner1x, coef2x, near3x, near2y, coef3y, halo_v):
+        done.sent(dummy)
 
     near3y.arrived(dummy)
     line = lanes((16, 128))
@@ -487,9 +526,10 @@
         return jnp.concatenate([pick(low, half_rows, 0), pick(high, half_rows + 4, 0)], axis=0)
 
     lifted = [onto2(x) for x in range(-3, 4)]
-    near2y.arrived(dummy)
+    near2x.arrived(dummy)
     for x in range(X2):
-        P2[x] = F2[1, x] + lifted[x // 2]
+        F2[0, x], value = unpacked(T2[x])
+        P2[x] = value + lifted[x // 2]
     sweep(P2, Q2, c2, face(F2, 0), W2, 1, X2 - 1)
     sweep(Q2, P2, c2, face(F2, 0), W2, 2, X2 - 2)
     sweep(P2, Q2, c2, face(F2, 0), W2, 3, X2 - 3)
@@ -530,7 +570,7 @@
             out[x, :, part] = jnp.where(is_even, pick(halves[0], index, 1), pick(halves[1], index, 1))
 
     near3y.sent(dummy)
-    near2y.sent(dummy)
+    near2x.sent(dummy)
 
 
 def solution(mesh):
@@ -543,21 +583,22 @@
         return pl.pallas_call(
             functools.partial(kernel, nx, ny),
             out_shape=jax.ShapeDtypeStruct((8, 8, 256), F32),
-            in_specs=[pl.BlockSpec(memory_space=pltpu.VMEM)] * 5,
+            in_specs=[pl.BlockSpec(memory_space=pltpu.HBM)] * 5,
             out_specs=pl.BlockSpec(memory_space=pltpu.VMEM),
             scratch_shapes=[
+                vmem(5, 8, 8, 256), pltpu.SemaphoreType.DMA((5,)),
                 vmem(5, X0 + 1, 16, 256), vmem(8, 8, 256), vmem(8, 8, 256), vmem(8, 256), vmem(8, 8, 256),
                 vmem(8, 8, 256), vmem(X0, 16, 256), vmem(X0, 16, 256), vmem(X0, 16, 256), vmem(X0, 16, 256),
                 vmem(5, X1 + 1, 24, 128), vmem(X1, 24, 128), vmem(X1, 24, 128), vmem(X1, 24, 128),
                 vmem(6, 14, 16, 128), vmem(2, 14, 16, 128),
-                vmem(6, X2, 16, 128), vmem(X2, 16, 128), vmem(8, 16, 128), vmem(X2, 16, 128), vmem(X2, 16, 128),
+                vmem(6, X2, 16, 128), vmem(2, X2, 16, 128), vmem(X2, 16, 128), vmem(X2, 16, 128), vmem(8, 16, 128), vmem(X2, 16, 128), vmem(X2, 16, 128),
                 vmem(SLOTS, 1, 128), vmem(4, SLOTS, 1, 128), vmem(GROUPS, 8, 128), vmem(4, GROUPS, 8, 128),
                 vmem(5, GROUPS, 16, 128), vmem(GROUPS, 16, 128), vmem(GROUPS, 16, 128), vmem(GROUPS, 16, 128),
                 vmem(8192, 128),
-                pltpu.SemaphoreType.DMA((13,)), pltpu.SemaphoreType.DMA((13,)),
+                pltpu.SemaphoreType.DMA((16,)), pltpu.SemaphoreType.DMA((16,)),
             ],
             compiler_params=pltpu.CompilerParams(
-                collective_id=0, has_side_effects=True, vmem_limit_bytes=40 * 2**20
+                collective_id=0, has_side_effects=True, vmem_limit_bytes=64 * 2**20
             ),
         )(*args)
 

time: 58.7 us -> 47.4 us (0.81); the launches traced: 57.7 us -> 47.2 us
  Pallas kernels: 52.9 us -> 45.7 us
  local copies, waits for them, and re-layouts: 4.83 us -> 1.47 us
    pallas_call x1, Pallas kernels: 52.9 us -> 45.7 us  [body(): pl.pallas_call(functools.partial(kernel, nx, ny), out_shape=jax.ShapeDtyp...]
    unnamed x11 -> x1, local copies, waits for them, and re-layouts: 4.83 us -> 1.47 us
where the time goes in v2:
time: 47.4 us; the launch traced here: 47.2 us
  Pallas kernels  45.7 us (96%)
  local copies, waits for them, and re-layouts  1.47 us (3%)
    pallas_call x1, Pallas kernels, body(): pl.pallas_call(functools.partial(kernel, nx, ny), out_shape=jax.ShapeDtyp...  45.7 us
    unnamed x1, local copies, waits for them, and re-layouts  1.47 us

profile of v2, /device:TPU:1, one launch (start us, length us, event | category | flops | bytes accessed | tf_op | source)
XLA Modules:
  0.0 47.2 jit_solution(16783592430030374308)
XLA Ops:
  0.0 45.7 %shard_map.55 = f32[8,8,256]{2,1,0:T(8,128)} custom-call(f32[8,8,256]{2,1,0:T(8,128)} %rhs.1, f32[8,8,256]{2,1,0:T(8,128)} %acoef.1, f32[8,8,256]{2,1,0:T(8,128)} %beta_x.1, f32[8,8,256]{2,1,0:T(8,128)} %beta_y.1, f32[8,8,256]{2,1,0:T(8,128)} %beta_z.1), custom_call_target="tpu_custom_call" | custom-call | tf_op jit(solution)/shard_map/pallas_call | solution.py:583
  45.7 1.5 %copy.7 = f32[8,8,256]{2,1,0:T(8,128)} copy(f32[8,8,256]{2,1,0:T(8,128)} %shard_map.55) | data formatting | bytes 131072

commit v3 on v2

--- a/solution.py
+++ b/solution.py
@@ -30,17 +30,30 @@
     return 0 if offset == 0 else size * (abs(offset) - 1) + 1
 
 
-AROUND = [(a, b) for a in (-1, 0, 1) for b in (-1, 0, 1) if (a, b) != (0, 0)]
-WIDE = [
-    (a, b)
-    for a in range(-3, 4)
-    for b in range(-3, 4)
-    if (a, b) != (0, 0) and gap(a, 4) + gap(b, 4) <= H1
-]
-ALONG_X = [a for a in range(-H3, H3 + 1) if a]
-ALONG_Y = list(range(1, 16))
-NEAR = [-3, -2, -1, 1, 2, 3]
-PARTNERS = sorted(set(WIDE) | {(a, 0) for a in ALONG_X} | {(0, b if b <= 8 else b - 16) for b in ALONG_Y})
+def distance(offset):
+    dx, dy = abs(offset[0]), offset[1] % 16
+    return dx / 2 + min(dy % 4, 4 - dy % 4) + min(dy / 4, 4 - dy / 4)
+
+
+def farthest_first(offsets):
+    return sorted(offsets, key=distance, reverse=True)
+
+
+AROUND = farthest_first([(a, b) for a in (-1, 0, 1) for b in (-1, 0, 1) if (a, b) != (0, 0)])
+WIDE = farthest_first(
+    [
+        (a, b)
+        for a in range(-3, 4)
+        for b in range(-3, 4)
+        if (a, b) != (0, 0) and gap(a, 4) + gap(b, 4) <= H1
+    ]
+)
+ALONG_X = [dx for dx, _ in farthest_first([(a, 0) for a in range(-H3, H3 + 1) if a])]
+ALONG_Y = [dy for _, dy in farthest_first([(0, b) for b in range(1, 16)])]
+NEAR = [-2, 2, -3, 3, -1, 1]
+PARTNERS = farthest_first(
+    sorted(set(WIDE) | {(a, 0) for a in ALONG_X} | {(0, b if b <= 8 else b - 16) for b in ALONG_Y})
+)
 
 
 def lanes(shape=(8, 128)):
@@ -126,7 +139,7 @@
 
 
 def kernel(nx, ny, rhs, acoef, beta_x, beta_y, beta_z, out,
-           IN, in_sems, F0, A0, E0, HX, HY, D0, W0, VA, VB, VP,
+           IN, in_sems, F0, A0, E0, HX, HY, D0, G0, W0, VA, VB, VP,
            F1, W1, P1, Q1, G1, U1,
            F2, S2, T2, W2, FP, P2, Q2,
            R3, RC, PK, PC, F3, W3, P3, Q3,
@@ -186,44 +199,13 @@
             A0[x, :, part] = a[half]
             E0[x, :, part] = extra
 
-    pl.semaphore_wait(barrier, len(PARTNERS))
-
-    faces = group(0)
-    faces.start(F0.at[2, H0, own], HX.at[:, :], (-1, 0))
-    faces.start(F0.at[3, pl.ds(H0, 8), pl.ds(0, 1)], HY.at[:, pl.ds(0, 1)], (0, -1))
-    halo = group(1)
-
-    def span_x(offset, wide):
-        if offset == 0:
-            return pl.ds(H0, 8), pl.ds(H0, 8)
-        if offset < 0:
-            return pl.ds(H0, wide), pl.ds(H0 + 8, wide)
-        return pl.ds(H0 + 8 - wide, wide), pl.ds(H0 - wide, wide)
-
-    def span_y(offset, wide):
-        if offset == 0:
-            return pl.ds(0, 8), pl.ds(0, 8)
-        if offset < 0:
-            return pl.ds(0, wide), pl.ds(8, wide)
-        return pl.ds(8 - wide, wide), pl.ds(16 - wide, wide)
-
-    def spans(dx, dy):
-        width = 2 if dx != 0 and dy != 0 else 3
-        sx, tx = span_x(dx, width)
-        sy, ty = span_y(dy, width)
-        return sx, sy, tx, ty
-
-    for dx, dy in AROUND:
-        sx, sy, tx, ty = spans(dx, dy)
-        halo.start(F0.at[:, sx, sy], F0.at[:, tx, ty], (dx, dy))
-    halo.start(F0.at[2, H0 + 3, own], F0.at[2, H0 + 11, own], (-1, 0))
-    halo.start(F0.at[3, pl.ds(H0, 8), pl.ds(3, 1)], F0.at[3, pl.ds(H0, 8), pl.ds(11, 1)], (0, -1))
-    for dx, dy, number, x, y in (
-        (-1, -1, 2, 2, 0), (-1, -1, 3, 2, 0), (-1, -1, 2, 0, 2), (-1, -1, 3, 0, 2),
-        (-1, 1, 2, 2, 7), (-1, 1, 2, 0, 5), (1, -1, 3, 7, 2), (1, -1, 3, 5, 0),
-    ):
-        source = F0.at[number, H0 + x, pl.ds(y, 1)]
-        halo.start(source, F0.at[number, H0 + x - 8 * dx, pl.ds((y - 8 * dy) % 16, 1)], (dx, dy))
+    for x in range(8):
+        for half, part in ((0, E), (1, O)):
+            bx, by, bz = (F0[n, H0 + x, own, part] for n in (2, 3, 4))
+            total = F0[1, H0 + x, own, part] + bx + by + up(by) + bz
+            if x < 7:
+                total = total + F0[2, H0 + x + 1, own, part]
+            D0[x, :, part] = total + (F0[4, H0 + x, own, O] if half == 0 else right(F0[4, H0 + x, own, E]))
 
     def both(get):
         return [get(x, E) + get(x, O) for x in range(8)]
@@ -253,6 +235,56 @@
     def send1(numbers, offset, collection):
         sx, sy, tx, ty = wide_spans(*offset)
         collection.start(F1.at[numbers, sx, sy], F1.at[numbers, tx, ty], offset)
+
+    pl.semaphore_wait(barrier, len(PARTNERS))
+
+    faces = group(0)
+    faces.start(F0.at[2, H0, own], HX.at[:, :], (-1, 0))
+    faces.start(F0.at[3, pl.ds(H0, 8), pl.ds(0, 1)], HY.at[:, pl.ds(0, 1)], (0, -1))
+    halo = group(1)
+
+    def span_x(offset, wide):
+        if offset == 0:
+            return pl.ds(H0, 8), pl.ds(H0, 8)
+        if offset < 0:
+            return pl.ds(H0, wide), pl.ds(H0 + 8, wide)
+        return pl.ds(H0 + 8 - wide, wide), pl.ds(H0 - wide, wide)
+
+    def span_y(offset, wide):
+        if offset == 0:
+            return pl.ds(0, 8), pl.ds(0, 8)
+        if offset < 0:
+            return pl.ds(0, wide), pl.ds(8, wide)
+        return pl.ds(8 - wide, wide), pl.ds(16 - wide, wide)
+
+    def spans(dx, dy):
+        width = 2 if dx != 0 and dy != 0 else 3
+        sx, tx = span_x(dx, width)
+        sy, ty = span_y(dy, width)
+        return sx, sy, tx, ty
+
+    for dx, dy, number, x, y in (
+        (-1, -1, 2, 2, 0), (-1, -1, 3, 2, 0), (-1, -1, 2, 0, 2), (-1, -1, 3, 0, 2),
+        (-1, 1, 2, 2, 7), (-1, 1, 2, 0, 5), (1, -1, 3, 7, 2), (1, -1, 3, 5, 0),
+    ):
+        source = F0.at[number, H0 + x, pl.ds(y, 1)]
+        halo.start(source, F0.at[number, H0 + x - 8 * dx, pl.ds((y - 8 * dy) % 16, 1)], (dx, dy))
+    for dx, dy in AROUND:
+        if dx and dy:
+            sx, sy, tx, ty = spans(dx, dy)
+            halo.start(F0.at[:, sx, sy], F0.at[:, tx, ty], (dx, dy))
+    planes = pl.ds(H0, 8)
+    for dy in (-1, 1):
+        near, far, there, beyond = (0, 2, 8, 10) if dy < 0 else (6, 5, 14, 13)
+        halo.start(F0.at[:, planes, pl.ds(near, 2)], F0.at[:, planes, pl.ds(there, 2)], (0, dy))
+        halo.start(F0.at[0, planes, pl.ds(far, 1)], F0.at[0, planes, pl.ds(beyond, 1)], (0, dy))
+        halo.start(D0.at[:, pl.ds(far, 1)], F0.at[1, planes, pl.ds(beyond, 1)], (0, dy))
+        if dy < 0:
+            halo.start(F0.at[3, planes, pl.ds(far, 1)], F0.at[3, planes, pl.ds(beyond, 1)], (0, dy))
+    for dx in (-1, 1):
+        sx, sy, tx, ty = spans(dx, 0)
+        halo.start(F0.at[:, sx, sy], F0.at[:, tx, ty], (dx, 0))
+    halo.start(F0.at[2, H0 + 3, own], F0.at[2, H0 + 11, own], (-1, 0))
 
     faces1y = group(2)
     for dy in NEAR:
@@ -315,11 +347,17 @@
             by = F0[3, x, :, part]
             total = F0[1, x, :, part] + F0[2, x, :, part] + F0[2, x + 1, :, part] + by + up(by) + hz[half]
             total = total + (hz[1] if half == 0 else right(hz[0]))
+            if H0 <= x < H0 + 8:
+                known = F0[1, x, pl.ds(8, 8), part]
+                if x == H0 + 7:
+                    known = known + F0[2, x + 1, pl.ds(8, 8), part]
+                outer = jnp.where((row == 2) | (row == 5), known, total[8:16])
+                total = jnp.concatenate([total[0:8], outer], axis=0)
             w = 0.8 / total
             W0[x, :, part] = w
             VA[x, :, part] = w * F0[0, x, :, part]
             if H0 <= x < H0 + 8:
-                D0[x - H0, :, part] = total[0:8]
+                G0[x - H0, :, part] = total[0:8]
 
     def couplings0(src, x, count=16):
         ve, vo = src[x, :, E], src[x, :, O]
@@ -345,7 +383,7 @@
         parts = []
         for v, total, part in couplings0(VA, H0 + x):
             v, total = v[0:8], total[0:8]
-            parts.append(F0[0, H0 + x, own, part] + total - D0[x, :, part] * v)
+            parts.append(F0[0, H0 + x, own, part] + total - G0[x, :, part] * v)
             VP[H0 + x, own, part] = v
         remains.append(parts[0] + parts[1])
     f1 = coarsen(remains, "c")
@@ -582,13 +620,13 @@
     def body(*args):
         return pl.pallas_call(
             functools.partial(kernel, nx, ny),
-            out_shape=jax.ShapeDtypeStruct((8, 8, 256), F32),
+            out_shape=pltpu.VMEM((8, 8, 256), F32),
             in_specs=[pl.BlockSpec(memory_space=pltpu.HBM)] * 5,
             out_specs=pl.BlockSpec(memory_space=pltpu.VMEM),
             scratch_shapes=[
                 vmem(5, 8, 8, 256), pltpu.SemaphoreType.DMA((5,)),
                 vmem(5, X0 + 1, 16, 256), vmem(8, 8, 256), vmem(8, 8, 256), vmem(8, 256), vmem(8, 8, 256),
-                vmem(8, 8, 256), vmem(X0, 16, 256), vmem(X0, 16, 256), vmem(X0, 16, 256), vmem(X0, 16, 256),
+                vmem(8, 8, 256), vmem(8, 8, 256), vmem(X0, 16, 256), vmem(X0, 16, 256), vmem(X0, 16, 256), vmem(X0, 16, 256),
                 vmem(5, X1 + 1, 24, 128), vmem(X1, 24, 128), vmem(X1, 24, 128), vmem(X1, 24, 128),
                 vmem(6, 14, 16, 128), vmem(2, 14, 16, 128),
                 vmem(6, X2, 16, 128), vmem(2, X2, 16, 128), vmem(X2, 16, 128), vmem(X2, 16, 128), vmem(8, 16, 128), vmem(X2, 16, 128), vmem(X2, 16, 128),
@@ -598,7 +636,7 @@
                 pltpu.SemaphoreType.DMA((16,)), pltpu.SemaphoreType.DMA((16,)),
             ],
             compiler_params=pltpu.CompilerParams(
-                collective_id=0, has_side_effects=True, vmem_limit_bytes=64 * 2**20
+                collective_id=0, has_side_effects=True, vmem_limit_bytes=60 * 2**20
             ),
         )(*args)
 

time: 47.4 us -> 44.9 us (0.947)
  Pallas kernels: 45.7 us -> 44.1 us
  local copies, waits for them, and re-layouts: 1.47 us -> 0.63 us
    pallas_call x1, Pallas kernels: 45.7 us -> 44.1 us  [body(): pl.pallas_call(functools.partial(kernel, nx, ny), out_shape=pltpu.VMEM((8...]
    unnamed x1, local copies, waits for them, and re-layouts: 1.47 us -> 0.63 us
where the time goes in v3:
time: 44.9 us; the launch traced here: 44.7 us
  Pallas kernels  44.1 us (98%)
  local copies, waits for them, and re-layouts  0.63 us (1%)
    pallas_call x1, Pallas kernels, body(): pl.pallas_call(functools.partial(kernel, nx, ny), out_shape=pltpu.VMEM((8...  44.1 us

profile of v3, /device:TPU:1, one launch (start us, length us, event | category | flops | bytes accessed | tf_op | source)
XLA Modules:
  0.0 44.7 jit_solution(12438905307504429352)
XLA Ops:
  0.0 44.1 %shard_map.55 = f32[8,8,256]{2,1,0:T(8,128)S(1)} custom-call(f32[8,8,256]{2,1,0:T(8,128)} %rhs.1, f32[8,8,256]{2,1,0:T(8,128)} %acoef.1, f32[8,8,256]{2,1,0:T(8,128)} %beta_x.1, f32[8,8,256]{2,1,0:T(8,128)} %beta_y.1, f32[8,8,256]{2,1,0:T(8,128)} %beta_z.1), custom_call_target="tpu_custom_call" | custom-call | tf_op jit(solution)/shard_map/pallas_call | solution.py:621
  44.1 0.6 %copy.7 = f32[8,8,256]{2,1,0:T(8,128)} copy(f32[8,8,256]{2,1,0:T(8,128)S(1)} %shard_map.55) | data formatting | bytes 131072

commit v4 on v3

--- a/solution.py
+++ b/solution.py
@@ -140,7 +140,7 @@
 
 def kernel(nx, ny, rhs, acoef, beta_x, beta_y, beta_z, out,
            IN, in_sems, F0, A0, E0, HX, HY, D0, G0, W0, VA, VB, VP,
-           F1, W1, P1, Q1, G1, U1,
+           F1, D1, W1, P1, Q1, G1, U1,
            F2, S2, T2, W2, FP, P2, Q2,
            R3, RC, PK, PC, F3, W3, P3, Q3,
            dummy, send_sems, recv_sems):
@@ -223,24 +223,27 @@
     e3 = [0.5 * t for t in coarsen(e2, "c", to32)]
     bx3, by3, bz3 = coarsen(bx2, "x", to32), coarsen(by2, "y", to32), coarsen(bz2, "z", to32)
 
-    for number, field in enumerate((bx1, by1, bz1)):
+    for number, field in enumerate(([a + e for a, e in zip(a1, e1)], bx1, by1, bz1)):
         for i in range(4):
-            F1[2 + number, H1 + i, pl.ds(0, 4)] = field[i][0:4]
-
-    def wide_spans(dx, dy):
-        fx, cx = reach(-dx, 4, H1)
-        fy, cy = reach(-dy, 4, H1)
+            F1[1 + number, H1 + i, pl.ds(0, 4)] = field[i][0:4]
+
+    def wide_spans(dx, dy, more=0):
+        fx, cx = reach(-dx, 4, H1 + (more if dx < 0 else 0))
+        fy, cy = reach(-dy, 4, H1 + (more if dy < 0 else 0))
         return pl.ds(H1 + fx, cx), pl.ds(fy, cy), pl.ds(H1 - 4 * dx + fx, cx), pl.ds((fy - 4 * dy) % 24, cy)
 
-    def send1(numbers, offset, collection):
-        sx, sy, tx, ty = wide_spans(*offset)
-        collection.start(F1.at[numbers, sx, sy], F1.at[numbers, tx, ty], offset)
+    def send1(offset, collection):
+        sx, sy, tx, ty = wide_spans(*offset, 1)
+        collection.start(F1.at[pl.ds(1, 4), sx, sy], F1.at[pl.ds(1, 4), tx, ty], offset)
 
     pl.semaphore_wait(barrier, len(PARTNERS))
 
     faces = group(0)
     faces.start(F0.at[2, H0, own], HX.at[:, :], (-1, 0))
     faces.start(F0.at[3, pl.ds(H0, 8), pl.ds(0, 1)], HY.at[:, pl.ds(0, 1)], (0, -1))
+    coef1y = group(2)
+    for dy in NEAR:
+        send1((0, dy), coef1y)
     halo = group(1)
 
     def span_x(offset, wide):
@@ -286,9 +289,9 @@
         halo.start(F0.at[:, sx, sy], F0.at[:, tx, ty], (dx, 0))
     halo.start(F0.at[2, H0 + 3, own], F0.at[2, H0 + 11, own], (-1, 0))
 
-    faces1y = group(2)
-    for dy in NEAR:
-        send1(pl.ds(2, 3), (0, dy), faces1y)
+    coef1x = group(4)
+    for dx in NEAR:
+        send1((dx, 0), coef1x)
 
     faces.arrived(dummy)
     hx = HX[:, E] + HX[:, O]
@@ -313,11 +316,8 @@
             result.append(a[i] + e[i] + bx[i] + high_x + by[i] + high_y + bz[i] + right(bz[i]))
         return result
 
-    d1 = diag_of(a1, e1, bx1, by1, bz1, hx1, hy1, 3)
     d2 = diag_of(a2, e2, bx2, by2, bz2, hx2, hy2, 1)
     d3 = diag_of(a3, e3, bx3, by3, bz3, hx3, [hy3], 0)
-    for i in range(4):
-        F1[1, H1 + i, pl.ds(0, 4)] = d1[i][0:4]
     two = pl.ds(0, 2)
     mid = pl.ds(H2, 2)
     for i in range(2):
@@ -327,18 +327,26 @@
     for number, field in enumerate((d3, bx3, by3, bz3)):
         RC[number, H3] = field[0][0:1]
 
-    diag1y = group(3)
-    for dy in NEAR:
-        send1(pl.ds(1, 1), (0, dy), diag1y)
-    coef1x = group(4)
-    for dx in NEAR:
-        send1(pl.ds(1, 4), (dx, 0), coef1x)
     coef2y = group(6)
     for dy in NEAR:
         coef2y.start(S2.at[:, mid, two], S2.at[:, mid, pl.ds((-2 * dy) % 16, 2)], (0, dy))
-    coef3x = group(8)
-    for dx in ALONG_X:
-        coef3x.start(RC.at[:, H3], RC.at[:, H3 - dx], (dx, 0))
+    coef1y.arrived(dummy)
+    corner1x = group(5)
+    for dx, parts in (
+        (-2, ((0, 4, 4, 4), (0, 4, 19, 5), (0, 1, 8, 1))),
+        (2, ((0, 4, 4, 4), (0, 4, 20, 4), (3, 1, 8, 1))),
+        (-1, ((0, 4, 4, 4), (0, 4, 8, 5), (0, 4, 16, 8), (0, 1, 15, 1))),
+        (1, ((0, 4, 4, 4), (0, 4, 8, 5), (0, 4, 16, 8))),
+        (-3, ((0, 1, 4, 1), (0, 1, 23, 1))),
+        (3, ((3, 1, 4, 1),)),
+    ):
+        for plane, planes_sent, first, count in parts:
+            span = pl.ds(first, count)
+            corner1x.start(
+                F1.at[pl.ds(1, 4), pl.ds(H1 + plane, planes_sent), span],
+                F1.at[pl.ds(1, 4), pl.ds(H1 + plane - 4 * dx, planes_sent), span],
+                (dx, 0),
+            )
 
     halo.arrived(dummy)
     for x in range(X0):
@@ -395,19 +403,6 @@
         sx, sy, tx, ty = wide_spans(*offset)
         wide_f.start(F1.at[0, sx, sy], F1.at[0, tx, ty], offset)
 
-    faces1y.arrived(dummy)
-    diag1y.arrived(dummy)
-    corner1x = group(5)
-    for dx in (-2, -1, 1, 2):
-        fx, cx = reach(-dx, 4, H1)
-        for first, count in ((4, 4), (20, 4)) if abs(dx) == 2 else ((4, 4), (8, 4), (16, 8)):
-            span = pl.ds(first, count)
-            corner1x.start(
-                F1.at[pl.ds(1, 4), pl.ds(H1 + fx, cx), span],
-                F1.at[pl.ds(1, 4), pl.ds(H1 - 4 * dx + fx, cx), span],
-                (dx, 0),
-            )
-
     def along_x2(collection, ref, lead):
         for dx in NEAR:
             for first, count in {1: ((0, 8), (10, 6)), 2: ((0, 5), (13, 3)), 3: ((0, 3), (15, 1))}[abs(dx)]:
@@ -417,6 +412,9 @@
     coef2y.arrived(dummy)
     coef2x = group(7)
     along_x2(coef2x, S2, (slice(None),))
+    coef3x = group(8)
+    for dx in ALONG_X:
+        coef3x.start(RC.at[:, H3], RC.at[:, H3 - dx], (dx, 0))
 
     def packed(get):
         result = []
@@ -433,15 +431,13 @@
         return result
 
     one = pl.ds(0, 1)
-    coef3x.arrived(dummy)
-    for number in range(4):
-        for g, value in enumerate(packed(lambda s: RC[number, s])):
-            PC[number, g, one] = value
-            F3[1 + number, g, one] = value
     coef1x.arrived(dummy)
     corner1x.arrived(dummy)
     for x in range(X1):
-        W1[x] = 0.8 / F1[1, x]
+        by, bz = F1[3, x], F1[4, x]
+        total = F1[1, x] + F1[2, x] + F1[2, x + 1] + by + up(by) + bz + right(bz)
+        D1[x] = total
+        W1[x] = 0.8 / total
     coef2x.arrived(dummy)
     wide_lanes = lanes((16, 128))
 
@@ -471,7 +467,7 @@
 
     def remains1(x):
         v, total = couplings(lambda p: P1[p], *c1, x)
-        return F1[0, x] + total - F1[1, x] * v
+        return F1[0, x] + total - D1[x] * v
 
     pairs = lax.rem(2 * row, 8)
     for i in range(8):
@@ -506,6 +502,11 @@
     near2y = group(11)
     for dy in NEAR:
         near2y.start(T2.at[mid, two], T2.at[mid, pl.ds((-2 * dy) % 16, 2)], (0, dy))
+    coef3x.arrived(dummy)
+    for number in range(4):
+        for g, value in enumerate(packed(lambda s: RC[number, s])):
+            PC[number, g, one] = value
+            F3[1 + number, g, one] = value
     coef3y = group(13)
     for dy in ALONG_Y:
         coef3y.start(PC.at[:, :, one], F3.at[pl.ds(1, 4), :, pl.ds(16 - dy, 1)], (0, dy))
@@ -534,7 +535,7 @@
     for g in range(GROUPS):
         W3[g] = 0.8 / F3[1, g]
     halo_v.arrived(dummy)
-    for done in (faces, halo, faces1y, diag1y, coef1x, coef2y, coef3x, wide_f, corner1x, coef2x, near3x, near2y, coef3y, halo_v):
+    for done in (faces, halo, coef1y, coef1x, coef2y, coef3x, wide_f, corner1x, coef2x, near3x, near2y, coef3y, halo_v):
         done.sent(dummy)
 
     near3y.arrived(dummy)
@@ -627,7 +628,7 @@
                 vmem(5, 8, 8, 256), pltpu.SemaphoreType.DMA((5,)),
                 vmem(5, X0 + 1, 16, 256), vmem(8, 8, 256), vmem(8, 8, 256), vmem(8, 256), vmem(8, 8, 256),
                 vmem(8, 8, 256), vmem(8, 8, 256), vmem(X0, 16, 256), vmem(X0, 16, 256), vmem(X0, 16, 256), vmem(X0, 16, 256),
-                vmem(5, X1 + 1, 24, 128), vmem(X1, 24, 128), vmem(X1, 24, 128), vmem(X1, 24, 128),
+                vmem(5, X1 + 1, 24, 128), vmem(X1, 24, 128), vmem(X1, 24, 128), vmem(X1, 24, 128), vmem(X1, 24, 128),
                 vmem(6, 14, 16, 128), vmem(2, 14, 16, 128),
                 vmem(6, X2, 16, 128), vmem(2, X2, 16, 128), vmem(X2, 16, 128), vmem(X2, 16, 128), vmem(8, 16, 128), vmem(X2, 16, 128), vmem(X2, 16, 128),
                 vmem(SLOTS, 1, 128), vmem(4, SLOTS, 1, 128), vmem(GROUPS, 8, 128), vmem(4, GROUPS, 8, 128),

time: 44.9 us -> 44.1 us (0.982)
  Pallas kernels: 44.1 us -> 43.3 us
    pallas_call x1, Pallas kernels: 44.1 us -> 43.3 us  [body(): pl.pallas_call(functools.partial(kernel, nx, ny), out_shape=pltpu.VMEM((8...]
where the time goes in v4:
time: 44.1 us; the launch traced here: 43.9 us
  Pallas kernels  43.3 us (98%)
  local copies, waits for them, and re-layouts  0.63 us (1%)
    pallas_call x1, Pallas kernels, body(): pl.pallas_call(functools.partial(kernel, nx, ny), out_shape=pltpu.VMEM((8...  43.3 us

profile of v4, /device:TPU:1, one launch (start us, length us, event | category | flops | bytes accessed | tf_op | source)
XLA Modules:
  0.0 43.9 jit_solution(5933322257893364993)
XLA Ops:
  0.0 43.3 %shard_map.55 = f32[8,8,256]{2,1,0:T(8,128)S(1)} custom-call(f32[8,8,256]{2,1,0:T(8,128)} %rhs.1, f32[8,8,256]{2,1,0:T(8,128)} %acoef.1, f32[8,8,256]{2,1,0:T(8,128)} %beta_x.1, f32[8,8,256]{2,1,0:T(8,128)} %beta_y.1, f32[8,8,256]{2,1,0:T(8,128)} %beta_z.1), custom_call_target="tpu_custom_call" | custom-call | tf_op jit(solution)/shard_map/pallas_call | solution.py:622
  43.3 0.6 %copy.7 = f32[8,8,256]{2,1,0:T(8,128)} copy(f32[8,8,256]{2,1,0:T(8,128)S(1)} %shard_map.55) | data formatting | bytes 131072

commit v5 on v4

--- a/solution.py
+++ b/solution.py
@@ -53,7 +53,7 @@
 NEAR = [-2, 2, -3, 3, -1, 1]
 PARTNERS = farthest_first(
     sorted(set(WIDE) | {(a, 0) for a in ALONG_X} | {(0, b if b <= 8 else b - 16) for b in ALONG_Y})
-)
+)[::-1]
 
 
 def lanes(shape=(8, 128)):

time: 44.1 us -> 44.3 us (level)
  no operation moved by 1% of the time
where the time goes in v5:
time: 44.3 us; the launch traced here: 44.2 us
  Pallas kernels  43.5 us (98%)
  local copies, waits for them, and re-layouts  0.63 us (1%)
    pallas_call x1, Pallas kernels, body(): pl.pallas_call(functools.partial(kernel, nx, ny), out_shape=pltpu.VMEM((8...  43.5 us

profile of v5, /device:TPU:1, one launch (start us, length us, event | category | flops | bytes accessed | tf_op | source)
XLA Modules:
  0.0 44.2 jit_solution(12958058264903494104)
XLA Ops:
  0.0 43.5 %shard_map.55 = f32[8,8,256]{2,1,0:T(8,128)S(1)} custom-call(f32[8,8,256]{2,1,0:T(8,128)} %rhs.1, f32[8,8,256]{2,1,0:T(8,128)} %acoef.1, f32[8,8,256]{2,1,0:T(8,128)} %beta_x.1, f32[8,8,256]{2,1,0:T(8,128)} %beta_y.1, f32[8,8,256]{2,1,0:T(8,128)} %beta_z.1), custom_call_target="tpu_custom_call" | custom-call | tf_op jit(solution)/shard_map/pallas_call | solution.py:622
  43.5 0.6 %copy.7 = f32[8,8,256]{2,1,0:T(8,128)} copy(f32[8,8,256]{2,1,0:T(8,128)S(1)} %shard_map.55) | data formatting | bytes 131072
